TPU v7x, 256 devices: a whole 4x4x8 slice. The times are simulated.
256 devices in a mesh: feat: 32 (over x, y, core), batch: 8 (over z).
Axes of the slice: x: 4, y: 4, z: 8, core: 2. Of those that a mesh axis runs over, the one named last changes fastest.
Arguments:
- node_features: bfloat16 [768, 32768], P('feat'), may hold values from -6 to 6
- first_weight: bfloat16 [768, 2, 1024], P('feat'), may hold values from -0.15625 to 0.15625
- second_weight: bfloat16 [2048, 1024], replicated, may hold values from -0.125 to 0.125
- target_nodes: int32 [8, 2048], P('batch'), may hold values from 0 to 32767
- outer_nodes: int32 [8, 2048, 16], P('batch'), may hold values from 0 to 32767
- outer_counts: int32 [8, 2048], P('batch'), may hold values from 1 to 16
- inner_nodes: int32 [8, 1024, 8], P('batch', 'feat'), may hold values from 0 to 63
- inner_counts: int32 [8, 1024], P('batch', 'feat'), may hold values from 1 to 8
- cotangent: bfloat16 [8, 1024, 1024], P('batch', 'feat'), may hold values from -6 to 6
Outputs:
- output_rows: bfloat16 [8, 1024, 1024], P('batch', 'feat')
- grad_second: float32 [2048, 1024], P(('feat', 'batch'))
- grad_first: float32 [768, 2, 1024], P('feat')
All inputs are finite; a program needn't handle non-finite values.
Results may differ from a plain program's by a relative error of at most 0.02.
Values may be sent and summed in bfloat16 or wider, within the bound.
No kernel may reach another device: no remote copies, remote signals or barrier semaphores. Data moves between devices by JAX's collectives and lax.ppermute only.
A program may use at most 128 MiB of HBM per device.

v0:
```python
import jax
import jax.numpy as jnp
from jax import lax
from jax.sharding import PartitionSpec as P


def silu_slope(values):
    sig = jax.nn.sigmoid(values)
    return sig * (1.0 + values * (1.0 - sig))


def body(
    node_features,
    first_weight,
    second_weight,
    target_nodes,
    outer_nodes,
    outer_counts,
    inner_nodes,
    inner_counts,
    cotangent,
):
    target_indices = target_nodes[0]
    outer = outer_nodes[0]
    outer_cnt = outer_counts[0]
    inner = inner_nodes[0]
    inner_cnt = inner_counts[0]
    upstream_gradient = cotangent[0]
    fan_outer = outer.shape[1]
    fan_inner = inner.shape[1]
    width = second_weight.shape[1]
    feature_count_total = lax.axis_size("feat")
    owner_rows = outer.shape[0] // feature_count_total
    second_rows = inner.shape[0]
    self_part = node_features[:, target_indices]
    neighbour_indices = node_features[:, outer]
    slots = jnp.arange(fan_outer, dtype=jnp.int32)
    valid_mask = (slots[None, :] < outer_cnt[:, None]).astype(jnp.bfloat16)
    neighbour_sum = jnp.einsum(
        "uqi,qi->uq", neighbour_indices, valid_mask, preferred_element_type=jnp.float32
    )
    averaged = (neighbour_sum / outer_cnt.astype(jnp.float32)[None, :]).astype(jnp.bfloat16)
    stacked = jnp.stack([self_part, averaged], axis=1)
    exchanged = lax.all_to_all(stacked, "feat", split_axis=2, concat_axis=0, tiled=True)
    part = exchanged
    pre = lax.dot_general(
        part,
        lax.all_gather(first_weight, "feat", axis=0, tiled=True),
        (((0, 1), (0, 1)), ((), ())),
        preferred_element_type=jnp.float32,
    )
    hidden = jax.nn.silu(pre).astype(jnp.bfloat16)
    inner_slots = jnp.arange(fan_inner, dtype=jnp.int32)
    inner_valid_mask = (inner_slots[None, :] < inner_cnt[:, None]).astype(jnp.float32)
    columns = jnp.arange(owner_rows, dtype=jnp.int32)
    tally = jnp.sum(
        (inner[:, :, None] == columns[None, None, :]).astype(jnp.float32)
        * inner_valid_mask[:, :, None],
        axis=1,
    )
    divisor = inner_cnt.astype(jnp.float32)[:, None]
    mean_rows = (
        jnp.dot(tally, hidden.astype(jnp.float32), precision=lax.Precision.HIGHEST) / divisor
    ).astype(jnp.bfloat16)
    joined = jnp.concatenate([hidden[:second_rows], mean_rows], axis=1)
    output = jnp.dot(joined, second_weight, preferred_element_type=jnp.float32).astype(jnp.bfloat16)
    part = joined
    grad_second = lax.psum_scatter(
        lax.dot_general(
            part, upstream_gradient, (((0,), (0,)), ((), ())), preferred_element_type=jnp.float32
        ),
        ("feat", "batch"),
        scatter_dimension=0,
        tiled=True,
    )
    grad_joined = lax.dot_general(
        upstream_gradient,
        second_weight,
        (((1,), (1,)), ((), ())),
        preferred_element_type=jnp.float32,
    )
    spread = lax.dot_general(
        tally,
        grad_joined[:, width:] / divisor,
        (((0,), (0,)), ((), ())),
        precision=lax.Precision.HIGHEST,
    )
    grad_hidden = spread + jnp.pad(grad_joined[:, :width], ((0, owner_rows - second_rows), (0, 0)))
    grad_pre = (grad_hidden * silu_slope(pre)).astype(jnp.bfloat16)
    slice_grad = lax.dot_general(
        stacked,
        lax.all_gather(grad_pre, "feat", axis=0, tiled=True),
        (((2,), (0,)), ((), ())),
        preferred_element_type=jnp.float32,
    )
    grad_first = lax.psum(slice_grad.astype(jnp.bfloat16), "batch").astype(jnp.float32)
    return (output[None], grad_second, grad_first)


def solution(mesh):
    in_specs = (
        P("feat", None),
        P("feat", None, None),
        P(),
        P("batch", None),
        P("batch", None, None),
        P("batch", None),
        P("batch", "feat", None),
        P("batch", "feat"),
        P("batch", "feat", None),
    )
    out_specs = (P("batch", "feat", None), P(("feat", "batch"), None), P("feat", None, None))
    return jax.shard_map(body, mesh=mesh, in_specs=in_specs, out_specs=out_specs, check_vma=False)
```

profile of v0, /device:TPU:0, one launch (start us, length us, event | category | flops | bytes accessed | tf_op | source)
XLA Modules:
  0.0 1586.3 jit_solution(13000676888692300973)
XLA Ops:
  7.2 1.5 copy.44
  8.8 7.5 copy.38
  16.3 0.3 copy.40
  16.6 0.3 reshape.104
  17.0 114.6 %gather_fusion.1 = bf16[32768,24]{1,0:T(8,128)(2,1)} fusion(bf16[24,32768]{0,1:T(8,128)(2,1)} %copy.38, s32[32768]{0:T(1024)S(1)} %broadcast_clamp_fusion), kind=kCustom, calls=%fused_computation.1 | custom fusion | bytes 3276800 | tf_op jit(solution)/shard_map/gather | solution.py:36
  131.6 0.3 fusion.11
  132.0 5.7 fusion.2
  137.7 0.5 copy.49
  138.2 10.1 gather_fusion
  148.3 0.2 copy.39
  148.6 0.7 copy.42
  149.3 2.1 reshape.115
  151.4 5.6 all-to-all-start
  157.0 0.2 all-gather.5.cloned.1.call-start
  157.2 0.1 copy.46
  157.3 3.5 fusion.15
  160.8 0.1 fusion.19
  160.9 0.1 select_reduce_fusion
  161.1 4.2 all-to-all-done
  165.3 1.5 reshape.116
  166.8 0.8 copy.43
  167.6 2.6 multiply_convert_fusion
  170.2 1.1 fusion.5
  171.4 0.0 all-reduce.3.cloned.1.call-start
  171.4 0.2 fusion.9
  171.6 50.3 %all-gather.5.cloned.1.call-done = bf16[2048,1024]{1,0:T(8,128)(2,1)} async-done(((bf16[64,1024]{1,0:T(8,128)(2,1)}), bf16[2048,1024]{1,0:T(8,128)(2,1)}) %all-gather.5.cloned.1.call-update) | async-done | bytes 4194320 | tf_op jit(solution)/shard_map/all_gather | solution.py:92
  222.0 3.7 fusion.6
  225.7 4.5 fusion.14
  230.2 3.6 fusion.10
  233.9 63.1 %all-reduce.3.cloned.1.call-done = bf16[24,2,1024]{2,0,1:T(8,128)(2,1)} async-done(((bf16[24,2,1024]{2,0,1:T(8,128)(2,1)}), bf16[24,2,1024]{2,0,1:T(8,128)(2,1)}) %all-reduce.3.cloned.1.call-update) | async-done | bytes 98320 | tf_op jit(solution)/shard_map/psum | solution.py:96
  297.0 1.7 copy.47
  298.7 1281.1 %reduce-scatter.2.cloned.1.call-done = f32[8,1024]{1,0:T(8,128)} async-done(((f32[2048,1024]{1,0:T(8,128)}), f32[8,1024]{1,0:T(8,128)}) %reduce-scatter.2.cloned.1.call-update) | async-done | bytes 32784 | tf_op jit(solution)/shard_map/reduce_scatter | solution.py:68
  (29 shorter events, 0.3 us)
Async XLA Ops:
  7.2 150.1 %copy-start = (bf16[1,32,1024]{2,1,0:T(8,128)(2,1)S(1)}, bf16[1,32,1024]{2,1,0:T(8,128)(2,1)}, u32[]{:S(2)}) copy-start(bf16[1,32,1024]{2,1,0:T(8,128)(2,1)} %param.17) | copy-start | bytes 196612
  7.2 160.4 %all-gather.3.cloned.1.call-start = ((), (), s32[]{:S(2)}) async-start(), calls=%async_computation.2 | async-start | bytes 3244032 | tf_op jit(solution)/shard_map/all_gather | solution.py:48
  8.8 7.5 copy-start.1
  8.8 8.1 copy-start.2
  132.0 6.2 copy-start.3
  137.7 19.5 %copy-start.4 = (s32[1,32,8]{1,2,0:T(8,128)S(1)}, s32[1,32,8]{1,2,0:T(8,128)}, u32[]{:S(2)}) copy-start(s32[1,32,8]{1,2,0:T(8,128)} %param.15) | copy-start | bytes 3076
  148.5 12.3 copy-start.5
  151.4 13.9 all-to-all-start
  157.0 65.0 %all-gather.5.cloned.1.call-start = ((), (), s32[]{:S(2)}) async-start(), calls=%async_computation.4 | async-start | bytes 4325376 | tf_op jit(solution)/shard_map/all_gather | solution.py:92
  171.4 125.6 %all-reduce.3.cloned.1.call-start = ((), (), s32[]{:S(2)}) async-start(), calls=%async_computation.5 | async-start | bytes 196608 | tf_op jit(solution)/shard_map/psum | solution.py:96
  225.7 1354.2 %reduce-scatter.2.cloned.1.call-start = ((), (), s32[]{:S(2)}) async-start(), calls=%async_computation.3 | async-start | bytes 8421376 | tf_op jit(solution)/shard_map/reduce_scatter | solution.py:68
Sparse Core Ops, SparseCore 0:
  10.6 51.3 all-gather.2
  171.5 50.4 all-gather.4
  225.8 71.1 all-reduce.2
  300.1 1279.6 reduce-scatter.1
where the time goes:
time: 1590 us
  waiting for transfers between devices  1400 us (88%)
  local copies, waits for them, and re-layouts  142 us (9%)
  matrix products  24.9 us (2%)
    reduce_scatter x1, waiting for transfers between devices, body(): lax.psum_scatter(lax.dot_general(part, upstream_gradient, (((0,), (0,)),...  1280 us
    gather x1, local copies, waits for them, and re-layouts, body(): neighbour_indices = node_features[:, outer]  115 us
    psum x1, waiting for transfers between devices, body(): lax.psum(slice_grad.astype(jnp.bfloat16), 'batch').astype(jnp.float32)  63.1 us
    all_gather x1, waiting for transfers between devices, body(): lax.all_gather(grad_pre, 'feat', axis=0, tiled=True)  50.3 us
  transfers between devices with their start and end apart: 5, of which 4 were waited for; matrix products, arithmetic and copies ran while one was open for 10% of the time, Pallas kernels for 0%

commit v1 on v0

v1 whole, which is shorter than its diff:
```python
import jax
import jax.numpy as jnp
from jax import lax
from jax.experimental import pallas as pl
from jax.experimental.pallas import tpu as pltpu
from jax.sharding import Mesh, PartitionSpec as P

BF16 = jnp.bfloat16
F32 = jnp.float32
LANES = 128


def gather_kernel(slots, owners, owners_y, owner_rows, slice_width, table_rows):
    def kernel(place_ref, index_ref, target_ref, own_ref, other_ref, count_ref, out_ref, relative_ref, table, rows):
        core, here = place_ref[0], place_ref[1]
        group_rows = owners * 2 * owner_rows
        lane = lax.broadcasted_iota(jnp.int32, (1, LANES), 1)
        is_self = (lane // slice_width) % 2 == 0
        tail = jnp.zeros((LANES - 4 * slice_width, LANES), F32)

        def turn(step, carry):
            for part in range(2):
                start = pl.multiple_of((step * 2 + part) * LANES, LANES)
                own = own_ref[:, pl.ds(start, LANES)].astype(F32)
                other = other_ref[:, pl.ds(start, LANES)].astype(F32)
                first = jnp.where(core == 0, own, other)
                second = jnp.where(core == 0, other, own)
                block = jnp.concatenate([first, first, second, second, tail], axis=0)
                table[pl.ds(start, LANES), :] = block.T
            return carry

        lax.fori_loop(0, table_rows // (2 * LANES), turn, 0)
        table[pl.ds(table_rows, 8), :] = jnp.zeros((8, LANES), F32)

        unroll = 8
        chunks = owner_rows // unroll

        def look_up(step, carry):
            owner = step // chunks
            source = (owner * 2 + core) * owner_rows + (step % chunks) * unroll
            for part in range(unroll):
                terms = [
                    table[pl.ds(index_ref[slot * group_rows + source + part], 1), :] for slot in range(slots)
                ]
                while len(terms) > 1:
                    terms = [a + b for a, b in zip(terms[::2], terms[1::2])]
                self_row = table[pl.ds(target_ref[source + part], 1), :]
                rows[pl.ds(step * unroll + part, 1), :] = jnp.where(is_self, self_row, terms[0])
            return carry

        lax.fori_loop(0, owners * chunks, look_up, 0)

        for owner in range(owners):
            source = pl.multiple_of((owner * 2 + core) * owner_rows, owner_rows)
            counts = jnp.broadcast_to(count_ref[pl.ds(source, owner_rows), :], (owner_rows, LANES))
            divisor = jnp.where(jnp.broadcast_to(is_self, (owner_rows, LANES)), 1.0, counts)
            values = rows[pl.ds(owner * owner_rows, owner_rows), :] / divisor
            values = values[:, : 4 * slice_width].astype(BF16)
            out_ref[owner] = values
            turn_y = lax.rem(owner % owners_y - here + owners_y, owners_y)
            relative_ref[turn_y, pl.ds(owner // owners_y * owner_rows, owner_rows), :] = values

    smem = pl.BlockSpec(memory_space=pltpu.SMEM)
    vmem = pl.BlockSpec(memory_space=pltpu.VMEM)
    return pl.pallas_call(
        kernel,
        out_shape=(
            jax.ShapeDtypeStruct((owners, owner_rows, 4 * slice_width), BF16),
            jax.ShapeDtypeStruct((owners_y, owners // owners_y * owner_rows, 4 * slice_width), BF16),
        ),
        in_specs=[smem, smem, smem, vmem, vmem, vmem],
        out_specs=(vmem, vmem),
        scratch_shapes=[
            pltpu.VMEM((table_rows + 8, LANES), F32),
            pltpu.VMEM((owners * owner_rows, LANES), F32),
        ],
        compiler_params=pltpu.CompilerParams(vmem_limit_bytes=48 << 20),
        cost_estimate=pl.CostEstimate(flops=50_000_000, bytes_accessed=100_000_000, transcendentals=0),
        name="gather_mean",
    )


def silu_slope(values):
    sig = jax.nn.sigmoid(values)
    return sig * (1.0 + values * (1.0 - sig))


def swap(values):
    return lax.ppermute(values, "core", [(0, 1), (1, 0)])


def exchange(values, axis):
    return lax.all_to_all(values, axis, split_axis=0, concat_axis=0, tiled=True)


def turn_blocks(blocks, axis):
    n = len(blocks)
    here = lax.axis_index(axis)
    got = [blocks[0]] + [lax.ppermute(blocks[k], axis, [(i, (i + k) % n) for i in range(n)]) for k in range(1, n)]
    return got, lambda got: jnp.stack(
        [lax.dynamic_index_in_dim(jnp.stack(got), (here - j) % n, 0, keepdims=False) for j in range(n)]
    )


def body(
    node_features,
    first_weight,
    second_weight,
    target_nodes,
    outer_nodes,
    outer_counts,
    inner_nodes,
    inner_counts,
    cotangent,
):
    nx, ny, nb = lax.axis_size("x"), lax.axis_size("y"), lax.axis_size("batch")
    core = lax.axis_index("core")
    slice_width, nodes = node_features.shape
    width = second_weight.shape[1]
    half = width // 2
    group_rows, slots = outer_nodes.shape[1:]
    owner_rows = group_rows // (nx * ny * 2)
    second_rows, fan_inner = inner_nodes.shape[1:]
    both = 2 * slice_width
    upstream = cotangent[0]

    weight = first_weight.transpose(1, 0, 2).reshape(both, width)
    kept = lax.dynamic_slice_in_dim(weight, core * half, half, axis=1)
    sent = swap(lax.dynamic_slice_in_dim(weight, (1 - core) * half, half, axis=1))
    pair = jnp.concatenate([jnp.where(core == 0, kept, sent), jnp.where(core == 0, sent, kept)], axis=0)
    weight_mine = exchange(jnp.broadcast_to(pair[None], (nx * ny,) + pair.shape), ("x", "y"))
    weight_mine = weight_mine.reshape(nx * ny * 2 * both, half)

    counts = outer_counts[0]
    live = jnp.arange(slots, dtype=jnp.int32)[:, None] < counts[None, :]
    index = jnp.where(live, outer_nodes[0].T, nodes).reshape(-1)
    other_features = swap(node_features)
    stacked, relative = gather_kernel(slots, nx * ny, ny, owner_rows, slice_width, nodes)(
        jnp.stack([core, lax.axis_index("y")]).astype(jnp.int32),
        index,
        target_nodes[0],
        node_features,
        other_features,
        counts.astype(F32)[:, None],
    )
    stacked, weight_mine = lax.optimization_barrier((stacked, weight_mine))
    weight_other = swap(weight_mine)
    owned = exchange(stacked, ("x", "y"))
    got, in_order = turn_blocks([relative[k] for k in range(ny)], "y")
    got[1], late_upstream = lax.optimization_barrier((got[1], upstream))
    along_y = in_order(got)
    owned = owned.transpose(1, 0, 2).reshape(owner_rows, nx * ny * 2 * both)
    pre_mine = jnp.dot(owned, weight_mine, preferred_element_type=F32)
    pre_other = jnp.dot(owned, weight_other, preferred_element_type=F32)
    pre = jnp.concatenate(
        [jnp.where(core == 0, pre_mine, pre_other), jnp.where(core == 0, pre_other, pre_mine)], axis=1
    )
    hidden = jax.nn.silu(pre).astype(BF16)

    inner = inner_nodes[0]
    inner_cnt = inner_counts[0]
    inner_live = (jnp.arange(fan_inner, dtype=jnp.int32)[None, :] < inner_cnt[:, None]).astype(F32)
    columns = jnp.arange(owner_rows, dtype=jnp.int32)
    tally = jnp.sum((inner[:, :, None] == columns[None, None, :]).astype(F32) * inner_live[:, :, None], axis=1)
    divisor = inner_cnt.astype(F32)[:, None]
    mean_rows = (jnp.dot(tally.astype(BF16), hidden, preferred_element_type=F32) / divisor).astype(BF16)
    joined = jnp.concatenate([hidden[:second_rows], mean_rows], axis=1)
    output = jnp.dot(joined, second_weight, preferred_element_type=F32).astype(BF16)
    grad_joined = lax.dot_general(late_upstream, second_weight, (((1,), (1,)), ((), ())), preferred_element_type=F32)
    spread = lax.dot_general(
        tally, grad_joined[:, width:] / divisor, (((0,), (0,)), ((), ())), precision=lax.Precision.HIGHEST
    )
    grad_hidden = spread + jnp.pad(grad_joined[:, :width], ((0, owner_rows - second_rows), (0, 0)))
    grad_pre = (grad_hidden * silu_slope(pre)).astype(BF16)

    chunk = 2 * width // nx
    columns_x = joined.reshape(second_rows, nx, chunk).transpose(1, 0, 2)
    columns_x = jnp.concatenate([columns_x[:, : second_rows // 2], columns_x[:, second_rows // 2 :]], axis=2)
    common = jnp.concatenate([grad_pre, upstream], axis=0)
    message = jnp.concatenate([jnp.broadcast_to(common[None], (nx,) + common.shape), columns_x], axis=1)
    message = exchange(message, "x")
    grad_pre_x = message[:, :owner_rows].reshape(nx * owner_rows, width)
    upstream_x = message[:, owner_rows : owner_rows + second_rows].reshape(nx * second_rows, width)
    columns_x = message[:, owner_rows + second_rows :]
    columns_x = jnp.concatenate([columns_x[:, :, :chunk], columns_x[:, :, chunk:]], axis=1)
    columns_x = columns_x.reshape(nx * second_rows, chunk)
    first_terms = lax.dot_general(
        along_y, grad_pre_x, (((1,), (0,)), ((), ())), preferred_element_type=F32
    ).reshape(ny, 2, both, width)

    kept = lax.dynamic_index_in_dim(first_terms, core, 1, keepdims=False)
    sent = swap(lax.dynamic_index_in_dim(first_terms, 1 - core, 1, keepdims=False).astype(BF16))
    piece = width // nb
    first_terms = (kept + sent.astype(F32)).astype(BF16).reshape(ny, both, nb, piece).transpose(0, 2, 1, 3)
    first_terms, columns_x = lax.optimization_barrier((first_terms.reshape(ny * nb, both, piece), columns_x))
    first_terms = exchange(first_terms, ("y", "batch"))
    first_piece = jnp.sum(first_terms.astype(F32), axis=0).astype(BF16)

    second_terms = lax.dot_general(
        columns_x, upstream_x, (((0,), (0,)), ((), ())), preferred_element_type=F32
    ).reshape(ny, 2, -1, width)
    kept = lax.dynamic_index_in_dim(second_terms, core, 1, keepdims=False)
    sent = swap(lax.dynamic_index_in_dim(second_terms, 1 - core, 1, keepdims=False).astype(BF16))
    second_terms = (kept + sent.astype(F32)).astype(BF16)
    here = lax.axis_index("y")
    got, _ = turn_blocks(
        [lax.dynamic_index_in_dim(second_terms, (here + k) % ny, 0, keepdims=False) for k in range(ny)], "y"
    )
    second_terms = sum(block.astype(F32) for block in got).astype(BF16)
    second_terms = second_terms.reshape(nb, -1, nb, piece).transpose(0, 2, 1, 3).reshape(nb, -1, piece)
    message = jnp.concatenate([jnp.broadcast_to(first_piece[None], (nb, both, piece)), second_terms], axis=1)
    message = exchange(message, "batch")
    grad_second = jnp.sum(message[:, both:].astype(F32), axis=0)
    grad_second = grad_second.reshape(nb, -1, piece).transpose(1, 0, 2).reshape(-1, width)
    grad_first = message[:, :both].reshape(nb, 2, slice_width, piece)
    grad_first = grad_first.transpose(2, 1, 0, 3).reshape(slice_width, 2, width)
    return (output[None], grad_second, grad_first.astype(F32))


def solution(mesh):
    feat, batch = mesh.devices.shape
    fine = Mesh(mesh.devices.reshape(4, feat // 8, 2, batch), ("x", "y", "core", "batch"))
    f = ("x", "y", "core")
    in_specs = (
        P(f, None),
        P(f, None, None),
        P(),
        P("batch", None),
        P("batch", None, None),
        P("batch", None),
        P("batch", f, None),
        P("batch", f),
        P("batch", f, None),
    )
    out_specs = (P("batch", f, None), P(("x", "y", "core", "batch"), None), P(f, None, None))
    return jax.shard_map(body, mesh=fine, in_specs=in_specs, out_specs=out_specs, check_vma=False)
```

time: 1590 us -> 136 us (0.09)
  the two profiles are of different devices: /device:TPU:0 before, /device:TPU:8 now
where the time goes in v1:
time: 136 us; the launch traced here: 134 us
  starting transfers between devices  45 us (33%)
  Pallas kernels  33.1 us (24%)
  waiting for transfers between devices  32.2 us (24%)
  matrix products  10.7 us (8%)
  local copies, waits for them, and re-layouts  7.65 us (6%)
  other arithmetic  4.14 us (3%)
    all_to_all x5, starting transfers between devices, exchange(): return lax.all_to_all(values, axis, split_axis=0, concat_axis=0, tiled=True)  35.3 us
    pallas_call x1, Pallas kernels, body(): gather_kernel(slots, nx * ny, ny, owner_rows, slice_width, nodes)  33.1 us
    all_to_all x5, waiting for transfers between devices, exchange(): return lax.all_to_all(values, axis, split_axis=0, concat_axis=0, tiled=True)  16.6 us
    ppermute x6, waiting for transfers between devices, turn_blocks(): lax.ppermute(blocks[k], axis, [(i, (i + k) % n) for i in range(n)])  13 us
    ppermute x6, starting transfers between devices, turn_blocks(): lax.ppermute(blocks[k], axis, [(i, (i + k) % n) for i in range(n)])  8.93 us
    dot_general x1, matrix products, body(): jnp.dot(joined, second_weight, preferred_element_type=F32).astype(BF16)  3.65 us
    dot_general x1, matrix products, body(): lax.dot_general(late_upstream, second_weight, (((1,), (1,)), ((), ())), p...  3.51 us
    unnamed x24, local copies, waits for them, and re-layouts  3.07 us
  transfers between devices with their start and end apart: 16, of which 11 were waited for; matrix products, arithmetic and copies ran while one was open for 9% of the time, Pallas kernels for 25%

profile of v1, /device:TPU:8, one launch (start us, length us, event | category | flops | bytes accessed | tf_op | source)
XLA Modules:
  0.0 134.0 jit_solution(6384664424750730466)
XLA Ops:
  0.6 0.9 copy.35
  2.2 0.7 collective-permute-done.1
  2.9 1.3 broadcast_in_dim.13
  4.2 7.5 %all-to-all-start = ((bf16[16,96,512]{2,1,0:T(8,128)(2,1)}), bf16[16,96,512]{2,1,0:T(8,128)(2,1)}, u32[]{:S(2)}, u32[]{:S(2)}) async-start(bf16[16,96,512]{2,1,0:T(8,128)(2,1)} %broadcast_in_dim.13), calls=%async_computation | async-start | bytes 3145728 | tf_op jit(solution)/shard_map/all_to_all | solution.py:93
  12.3 0.8 copy-done
  13.2 33.1 %gather_mean.1 = (bf16[16,64,96]{2,1,0:T(8,128)(2,1)}, bf16[4,256,96]{2,1,0:T(8,128)(2,1)S(1)}) custom-call(s32[2]{0:T(128)S(1)} %pad_add_fusion.place_ref, s32[32768]{0:T(1024)S(1)} %bitcast.115, s32[2048]{0:T(1024)S(1)} %bitcast.116, bf16[24,32768]{1,0:T(8,128)(2,1)S(1)} %copy-done, bf16[24,32768]{1,0:T(8,128)(2,1)} %collective-permute-done.other_ref, ...), custom_call_target="tpu_custom_call" | custom-call | flops 50000000 | bytes 100000000 | tf_op jit(solution)/shard_map/gather_mean/pallas_call | solution.py:138
  46.5 1.5 %collective-permute-start.3 = (bf16[256,96]{1,0:T(8,128)(2,1)S(1)}, bf16[256,96]{1,0:T(8,128)(2,1)S(1)}, u32[]{:S(2)}, u32[]{:S(2)}) collective-permute-start(bf16[256,96]{1,0:T(8,128)(2,1)S(1)} %get-tuple-element.37), channel_id=1, source_target_pairs={{0,16},{16,32},{32,48},{48,0},{1,17},{17,33},{33,49},{49,1},{2,18}... | collective-permute-start | bytes 147464 | tf_op jit(solution)/shard_map/ppermute | solution.py:99
  48.2 6.9 %all-to-all-start.1 = ((bf16[16,64,96]{2,1,0:T(8,128)(2,1)}), bf16[16,64,96]{2,1,0:T(8,128)(2,1)S(1)}, u32[]{:S(2)}, u32[]{:S(2)}) async-start(bf16[16,64,96]{2,1,0:T(8,128)(2,1)} %get-tuple-element.12), calls=%async_computation.1 | async-start | bytes 524288 | tf_op jit(solution)/shard_map/all_to_all | solution.py:93
  55.2 3.5 %fusion.21 = f32[32,2048]{1,0:T(8,128)S(1)} fusion(bf16[32,1024]{1,0:T(8,128)(2,1)S(1)} %bitcast.127, bf16[2048,1024]{1,0:T(8,128)(2,1)} %param.11), kind=kOutput, calls=%fused_computation.68 | convolution fusion | flops 134217728 | bytes 4521984 | tf_op jit(solution)/shard_map/dot_general | solution.py:169
  58.7 3.8 %all-to-all-done.1 = bf16[16,64,96]{2,1,0:T(8,128)(2,1)S(1)} async-done(((bf16[16,64,96]{2,1,0:T(8,128)(2,1)}), bf16[16,64,96]{2,1,0:T(8,128)(2,1)S(1)}, u32[]{:S(2)}, u32[]{:S(2)}) %all-to-all-start.1) | async-done | bytes 196640 | tf_op jit(solution)/shard_map/all_to_all | solution.py:93
  62.9 1.8 %fusion.20 = f32[64,512]{1,0:T(8,128)S(1)} fusion(bf16[64,1536]{1,0:T(8,128)(2,1)S(1)} %reshape.110, bf16[1536,512]{1,0:T(8,128)(2,1)} %bitcast.10), kind=kOutput, calls=%fused_computation.67 | convolution fusion | flops 100663296 | bytes 1900544 | tf_op jit(solution)/shard_map/dot_general | solution.py:153
  66.7 1.0 pad_maximum_fusion
  67.7 3.5 %all-to-all-start.2 = ((bf16[4,112,1024]{2,1,0:T(8,128)(2,1)}), bf16[4,112,1024]{2,1,0:T(8,128)(2,1)S(1)}, u32[]{:S(2)}, u32[]{:S(2)}) async-start(bf16[4,112,1024]{2,1,0:T(8,128)(2,1)} %pad_maximum_fusion), calls=%async_computation.2 | async-start | bytes 1835008 | tf_op jit(solution)/shard_map/all_to_all | solution.py:93
  71.2 1.7 %collective-permute-start.5 = (bf16[256,96]{1,0:T(8,128)(2,1)S(1)}, bf16[256,96]{1,0:T(8,128)(2,1)S(1)}, u32[]{:S(2)}, u32[]{:S(2)}) collective-permute-start(bf16[256,96]{1,0:T(8,128)(2,1)S(1)} %get-tuple-element.35), channel_id=1, source_target_pairs={{0,48},{16,0},{32,16},{48,32},{1,49},{17,1},{33,17},{49,33},{2,50}... | collective-permute-start | bytes 147464 | tf_op jit(solution)/shard_map/ppermute | solution.py:99
  73.0 0.9 collective-permute-start.4
  73.8 1.9 %collective-permute-done.5 = bf16[256,96]{1,0:T(8,128)(2,1)S(1)} collective-permute-done((bf16[256,96]{1,0:T(8,128)(2,1)S(1)}, bf16[256,96]{1,0:T(8,128)(2,1)S(1)}, u32[]{:S(2)}, u32[]{:S(2)}) %collective-permute-start.5) | collective-permute-done | bytes 49184 | tf_op jit(solution)/shard_map/ppermute | solution.py:99
  75.7 3.0 %collective-permute-done.4 = bf16[256,96]{1,0:T(8,128)(2,1)S(1)} collective-permute-done((bf16[256,96]{1,0:T(8,128)(2,1)S(1)}, bf16[256,96]{1,0:T(8,128)(2,1)S(1)}, u32[]{:S(2)}, u32[]{:S(2)}) %collective-permute-start.4) | collective-permute-done | bytes 49184 | tf_op jit(solution)/shard_map/ppermute | solution.py:99
  79.1 5.2 %all-to-all-done.2 = bf16[4,112,1024]{2,1,0:T(8,128)(2,1)S(1)} async-done(((bf16[4,112,1024]{2,1,0:T(8,128)(2,1)}), bf16[4,112,1024]{2,1,0:T(8,128)(2,1)S(1)}, u32[]{:S(2)}, u32[]{:S(2)}) %all-to-all-start.2) | async-done | bytes 917536 | tf_op jit(solution)/shard_map/all_to_all | solution.py:93
  84.7 0.8 fusion.7
  85.5 1.9 %collective-permute-done.6 = bf16[4,48,1024]{2,1,0:T(8,128)(2,1)S(1)} collective-permute-done((bf16[4,48,1024]{2,1,0:T(8,128)(2,1)}, bf16[4,48,1024]{2,1,0:T(8,128)(2,1)S(1)}, u32[]{:S(2)}, u32[]{:S(2)}) %collective-permute-start.6) | collective-permute-done | bytes 393248 | tf_op jit(solution)/shard_map/ppermute | solution.py:89
  87.4 0.8 copy_bitcast_fusion
  88.8 0.9 fusion.6
  89.8 11.2 %all-to-all-start.3 = ((bf16[32,48,128]{2,1,0:T(8,128)(2,1)}), bf16[32,48,128]{2,1,0:T(8,128)(2,1)S(1)}, u32[]{:S(2)}, u32[]{:S(2)}) async-start(bf16[32,48,128]{2,1,0:T(8,128)(2,1)} %bitcast.31), calls=%async_computation.3 | async-start | bytes 786432 | tf_op jit(solution)/shard_map/all_to_all | solution.py:93
  101.5 2.7 %collective-permute-start.9 = (bf16[64,1024]{1,0:T(8,128)(2,1)S(1)}, bf16[64,1024]{1,0:T(8,128)(2,1)S(1)}, u32[]{:S(2)}, u32[]{:S(2)}) collective-permute-start(bf16[64,1024]{1,0:T(8,128)(2,1)S(1)} %get-tuple-element.29), channel_id=1, source_target_pairs={{0,32},{16,48},{32,0},{48,16},{1,33},{17,49},{33,1},{49,17},{2,34}... | collective-permute-start | bytes 393224 | tf_op jit(solution)/shard_map/ppermute | solution.py:99
  104.2 1.8 %collective-permute-start.8 = (bf16[64,1024]{1,0:T(8,128)(2,1)S(1)}, bf16[64,1024]{1,0:T(8,128)(2,1)S(1)}, u32[]{:S(2)}, u32[]{:S(2)}) collective-permute-start(bf16[64,1024]{1,0:T(8,128)(2,1)S(1)} %get-tuple-element.27), channel_id=1, source_target_pairs={{0,16},{16,32},{32,48},{48,0},{1,17},{17,33},{33,49},{49,1},{2,18}... | collective-permute-start | bytes 393224 | tf_op jit(solution)/shard_map/ppermute | solution.py:99
  106.1 2.1 %collective-permute-done.10 = bf16[64,1024]{1,0:T(8,128)(2,1)S(1)} collective-permute-done((bf16[64,1024]{1,0:T(8,128)(2,1)S(1)}, bf16[64,1024]{1,0:T(8,128)(2,1)S(1)}, u32[]{:S(2)}, u32[]{:S(2)}) %collective-permute-start.10) | collective-permute-done | bytes 131104 | tf_op jit(solution)/shard_map/ppermute | solution.py:99
  108.2 5.6 %collective-permute-done.9 = bf16[64,1024]{1,0:T(8,128)(2,1)S(1)} collective-permute-done((bf16[64,1024]{1,0:T(8,128)(2,1)S(1)}, bf16[64,1024]{1,0:T(8,128)(2,1)S(1)}, u32[]{:S(2)}, u32[]{:S(2)}) %collective-permute-start.9) | collective-permute-done | bytes 131104 | tf_op jit(solution)/shard_map/ppermute | solution.py:99
  114.6 0.7 pad_maximum_fusion.3
  115.3 6.2 %all-to-all-start.4 = ((bf16[8,112,128]{2,1,0:T(8,128)(2,1)}), bf16[8,112,128]{2,1,0:T(8,128)(2,1)S(1)}, u32[]{:S(2)}, u32[]{:S(2)}) async-start(bf16[8,112,128]{2,1,0:T(8,128)(2,1)} %pad_maximum_fusion.3), calls=%async_computation.4 | async-start | bytes 458752 | tf_op jit(solution)/shard_map/all_to_all | solution.py:93
  121.5 3.6 %fusion.3 = bf16[1,32,1024]{2,1,0:T(8,128)(2,1)} fusion(bf16[2048,1024]{1,0:T(8,128)(2,1)} %param.11, bf16[32,1024]{1,0:T(8,128)(2,1)S(1)} %fusion.2, bf16[32,1024]{1,0:T(8,128)(2,1)S(1)} %slice.63), kind=kOutput, calls=%fused_computation.6 | convolution fusion | flops 134512640 | bytes 4390912 | tf_op jit(solution)/shard_map/dot_general | solution.py:168
  125.1 7.3 %all-to-all-done.4 = bf16[8,112,128]{2,1,0:T(8,128)(2,1)S(1)} async-done(((bf16[8,112,128]{2,1,0:T(8,128)(2,1)}), bf16[8,112,128]{2,1,0:T(8,128)(2,1)S(1)}, u32[]{:S(2)}, u32[]{:S(2)}) %all-to-all-start.4) | async-done | bytes 229408 | tf_op jit(solution)/shard_map/all_to_all | solution.py:93
  132.5 0.8 reshape.126
  (82 shorter events, 7.2 us)
Async XLA Ops:
  1.6 1.3 collective-permute-start.1
  1.7 10.7 %collective-permute-start = (bf16[24,32768]{1,0:T(8,128)(2,1)}, bf16[24,32768]{1,0:T(8,128)(2,1)}, u32[]{:S(2)}, u32[]{:S(2)}) collective-permute-start(bf16[24,32768]{1,0:T(8,128)(2,1)} %own_ref.1), channel_id=1, source_target_pairs={{0,8},{8,0},{1,9},{9,1},{2,10},{10,2},{3,11},{11,3},{4,12},{12,4},... | collective-permute-start | bytes 4718600 | tf_op jit(solution)/shard_map/ppermute | solution.py:89
  4.2 7.6 %copy-start.6 = (s32[1,2048,16]{1,2,0:T(8,128)S(1)}, s32[1,2048,16]{1,2,0:T(8,128)}, u32[]{:S(2)}) copy-start(s32[1,2048,16]{1,2,0:T(8,128)} %param.13) | copy-start | bytes 393220
  4.2 7.6 %copy-start.7 = (s32[1,2048]{1,0:T(1,128)S(1)}, s32[1,2048]{1,0:T(1,128)}, u32[]{:S(2)}) copy-start(s32[1,2048]{1,0:T(1,128)} %param.14) | copy-start | bytes 24580
  4.2 42.1 %all-to-all-start = ((bf16[16,96,512]{2,1,0:T(8,128)(2,1)}), bf16[16,96,512]{2,1,0:T(8,128)(2,1)}, u32[]{:S(2)}, u32[]{:S(2)}) async-start(bf16[16,96,512]{2,1,0:T(8,128)(2,1)} %broadcast_in_dim.13), calls=%async_computation | async-start | bytes 3145728 | tf_op jit(solution)/shard_map/all_to_all | solution.py:93
  11.8 1.4 %copy-start = (bf16[24,32768]{1,0:T(8,128)(2,1)S(1)}, bf16[24,32768]{1,0:T(8,128)(2,1)}, u32[]{:S(2)}) copy-start(bf16[24,32768]{1,0:T(8,128)(2,1)} %own_ref.1) | copy-start | bytes 4718596
  11.8 1.4 %copy-start.1 = (s32[1,2048]{1,0:T(1,128)S(1)}, s32[1,2048]{1,0:T(1,128)}, u32[]{:S(2)}) copy-start(s32[1,2048]{1,0:T(1,128)} %param.12) | copy-start | bytes 24580
  13.2 33.1 %copy-start.8 = (s32[1,32,8]{1,2,0:T(8,128)S(1)}, s32[1,32,8]{1,2,0:T(8,128)}, u32[]{:S(2)}) copy-start(s32[1,32,8]{1,2,0:T(8,128)} %param.15) | copy-start | bytes 3076
  13.2 33.2 %copy-start.9 = (s32[1,32]{1,0:T(1,128)S(1)}, s32[1,32]{1,0:T(1,128)}, u32[]{:S(2)}) copy-start(s32[1,32]{1,0:T(1,128)} %param.16) | copy-start | bytes 388
  13.2 42.0 %copy-start.5 = (bf16[1,32,1024]{2,1,0:T(8,128)(2,1)S(1)}, bf16[1,32,1024]{2,1,0:T(8,128)(2,1)}, u32[]{:S(2)}) copy-start(bf16[1,32,1024]{2,1,0:T(8,128)(2,1)} %param.17) | copy-start | bytes 196612
  46.3 18.4 %collective-permute-start.2 = (bf16[1536,512]{1,0:T(8,128)(2,1)}, bf16[1536,512]{1,0:T(8,128)(2,1)S(1)}, u32[]{:S(2)}, u32[]{:S(2)}) collective-permute-start(bf16[1536,512]{1,0:T(8,128)(2,1)} %bitcast.10), channel_id=1, source_target_pairs={{0,8},{8,0},{1,9},{9,1},{2,10},{10,2},{3,11},{11,3},{4,12},{12,4},... | collective-permute-start | bytes 4718600 | tf_op jit(solution)/shard_map/ppermute | solution.py:89
  46.5 8.6 %collective-permute-start.3 = (bf16[256,96]{1,0:T(8,128)(2,1)S(1)}, bf16[256,96]{1,0:T(8,128)(2,1)S(1)}, u32[]{:S(2)}, u32[]{:S(2)}) collective-permute-start(bf16[256,96]{1,0:T(8,128)(2,1)S(1)} %get-tuple-element.37), channel_id=1, source_target_pairs={{0,16},{16,32},{32,48},{48,0},{1,17},{17,33},{33,49},{49,1},{2,18}... | collective-permute-start | bytes 147464 | tf_op jit(solution)/shard_map/ppermute | solution.py:99
  48.2 14.3 %all-to-all-start.1 = ((bf16[16,64,96]{2,1,0:T(8,128)(2,1)}), bf16[16,64,96]{2,1,0:T(8,128)(2,1)S(1)}, u32[]{:S(2)}, u32[]{:S(2)}) async-start(bf16[16,64,96]{2,1,0:T(8,128)(2,1)} %get-tuple-element.12), calls=%async_computation.1 | async-start | bytes 524288 | tf_op jit(solution)/shard_map/all_to_all | solution.py:93
  58.7 6.1 %copy-start.3 = (f32[32,2048]{1,0:T(8,128)}, f32[32,2048]{1,0:T(8,128)S(1)}, u32[]{:S(2)}) copy-start(f32[32,2048]{1,0:T(8,128)S(1)} %fusion.21) | copy-start | bytes 786436
  65.1 1.0 copy-start.4
  65.2 1.0 slice-start.1
  67.7 16.5 %all-to-all-start.2 = ((bf16[4,112,1024]{2,1,0:T(8,128)(2,1)}), bf16[4,112,1024]{2,1,0:T(8,128)(2,1)S(1)}, u32[]{:S(2)}, u32[]{:S(2)}) async-start(bf16[4,112,1024]{2,1,0:T(8,128)(2,1)} %pad_maximum_fusion), calls=%async_computation.2 | async-start | bytes 1835008 | tf_op jit(solution)/shard_map/all_to_all | solution.py:93
  71.2 4.4 %collective-permute-start.5 = (bf16[256,96]{1,0:T(8,128)(2,1)S(1)}, bf16[256,96]{1,0:T(8,128)(2,1)S(1)}, u32[]{:S(2)}, u32[]{:S(2)}) collective-permute-start(bf16[256,96]{1,0:T(8,128)(2,1)S(1)} %get-tuple-element.35), channel_id=1, source_target_pairs={{0,48},{16,0},{32,16},{48,32},{1,49},{17,1},{33,17},{49,33},{2,50}... | collective-permute-start | bytes 147464 | tf_op jit(solution)/shard_map/ppermute | solution.py:99
  73.0 5.8 %collective-permute-start.4 = (bf16[256,96]{1,0:T(8,128)(2,1)S(1)}, bf16[256,96]{1,0:T(8,128)(2,1)S(1)}, u32[]{:S(2)}, u32[]{:S(2)}) collective-permute-start(bf16[256,96]{1,0:T(8,128)(2,1)S(1)} %get-tuple-element.36), channel_id=1, source_target_pairs={{0,32},{16,48},{32,0},{48,16},{1,33},{17,49},{33,1},{49,17},{2,34}... | collective-permute-start | bytes 147464 | tf_op jit(solution)/shard_map/ppermute | solution.py:99
  84.3 1.2 copy-start.2
  85.5 1.9 %collective-permute-start.6 = (bf16[4,48,1024]{2,1,0:T(8,128)(2,1)}, bf16[4,48,1024]{2,1,0:T(8,128)(2,1)S(1)}, u32[]{:S(2)}, u32[]{:S(2)}) collective-permute-start(bf16[4,48,1024]{2,1,0:T(8,128)(2,1)} %fusion.7), channel_id=1, source_target_pairs={{0,8},{8,0},{1,9},{9,1},{2,10},{10,2},{3,11},{11,3},{4,12},{12,4},... | collective-permute-start | bytes 1179656 | tf_op jit(solution)/shard_map/ppermute | solution.py:89
  85.5 2.9 %slice-start = ((bf16[4,112,1024]{2,1,0:T(8,128)(2,1)}), bf16[4,32,1024]{2,1,0:T(8,128)(2,1)S(1)}, s32[]{:S(2)}) async-start(bf16[4,112,1024]{2,1,0:T(8,128)(2,1)} %copy-done.2), calls=%async_computation.5 | async-start | bytes 524288 | tf_op jit(solution)/shard_map/slice | solution.py:183
  89.7 11.4 %collective-permute-start.7 = (bf16[4,64,1024]{2,1,0:T(8,128)(2,1)}, bf16[4,64,1024]{2,1,0:T(8,128)(2,1)S(1)}, u32[]{:S(2)}, u32[]{:S(2)}) collective-permute-start(bf16[4,64,1024]{2,1,0:T(8,128)(2,1)} %fusion.6), channel_id=1, source_target_pairs={{0,8},{8,0},{1,9},{9,1},{2,10},{10,2},{3,11},{11,3},{4,12},{12,4},... | collective-permute-start | bytes 1572872 | tf_op jit(solution)/shard_map/ppermute | solution.py:89
  89.8 24.7 %all-to-all-start.3 = ((bf16[32,48,128]{2,1,0:T(8,128)(2,1)}), bf16[32,48,128]{2,1,0:T(8,128)(2,1)S(1)}, u32[]{:S(2)}, u32[]{:S(2)}) async-start(bf16[32,48,128]{2,1,0:T(8,128)(2,1)} %bitcast.31), calls=%async_computation.3 | async-start | bytes 786432 | tf_op jit(solution)/shard_map/all_to_all | solution.py:93
  101.2 6.9 %collective-permute-start.10 = (bf16[64,1024]{1,0:T(8,128)(2,1)S(1)}, bf16[64,1024]{1,0:T(8,128)(2,1)S(1)}, u32[]{:S(2)}, u32[]{:S(2)}) collective-permute-start(bf16[64,1024]{1,0:T(8,128)(2,1)S(1)} %get-tuple-element.28), channel_id=1, source_target_pairs={{0,48},{16,0},{32,16},{48,32},{1,49},{17,1},{33,17},{49,33},{2,50}... | collective-permute-start | bytes 393224 | tf_op jit(solution)/shard_map/ppermute | solution.py:99
  101.5 12.2 %collective-permute-start.9 = (bf16[64,1024]{1,0:T(8,128)(2,1)S(1)}, bf16[64,1024]{1,0:T(8,128)(2,1)S(1)}, u32[]{:S(2)}, u32[]{:S(2)}) collective-permute-start(bf16[64,1024]{1,0:T(8,128)(2,1)S(1)} %get-tuple-element.29), channel_id=1, source_target_pairs={{0,32},{16,48},{32,0},{48,16},{1,33},{17,49},{33,1},{49,17},{2,34}... | collective-permute-start | bytes 393224 | tf_op jit(solution)/shard_map/ppermute | solution.py:99
  104.2 9.9 %collective-permute-start.8 = (bf16[64,1024]{1,0:T(8,128)(2,1)S(1)}, bf16[64,1024]{1,0:T(8,128)(2,1)S(1)}, u32[]{:S(2)}, u32[]{:S(2)}) collective-permute-start(bf16[64,1024]{1,0:T(8,128)(2,1)S(1)} %get-tuple-element.27), channel_id=1, source_target_pairs={{0,16},{16,32},{32,48},{48,0},{1,17},{17,33},{33,49},{49,1},{2,18}... | collective-permute-start | bytes 393224 | tf_op jit(solution)/shard_map/ppermute | solution.py:99
  115.3 17.1 %all-to-all-start.4 = ((bf16[8,112,128]{2,1,0:T(8,128)(2,1)}), bf16[8,112,128]{2,1,0:T(8,128)(2,1)S(1)}, u32[]{:S(2)}, u32[]{:S(2)}) async-start(bf16[8,112,128]{2,1,0:T(8,128)(2,1)} %pad_maximum_fusion.3), calls=%async_computation.4 | async-start | bytes 458752 | tf_op jit(solution)/shard_map/all_to_all | solution.py:93

commit v2 on v1

v2 whole, which is shorter than its diff:
```python
import jax
import jax.numpy as jnp
from jax import lax
from jax.experimental import pallas as pl
from jax.experimental.pallas import tpu as pltpu
from jax.sharding import Mesh, PartitionSpec as P

BF16 = jnp.bfloat16
F32 = jnp.float32
LANES = 128


def gather_kernel(slots, owners, owners_y, owner_rows, slice_width, table_rows, width):
    def kernel(place_ref, index_ref, target_ref, count_ref, own_ref, other_ref, out_ref, relative_ref, table, rows):
        core, here = place_ref[0], place_ref[1]
        group_rows = owners * 2 * owner_rows
        lane = lax.broadcasted_iota(jnp.int32, (1, LANES), 1)
        is_self = (lane // slice_width) % 2 == 0
        blocks = 16
        span = blocks * LANES
        tail = jnp.zeros((LANES - 4 * slice_width, span), F32)

        def turn(step, carry):
            start = pl.multiple_of(step * span, span)
            own = own_ref[:, pl.ds(start, span)].astype(F32)
            other = other_ref[:, pl.ds(start, span)].astype(F32)
            first = jnp.where(core == 0, own, other)
            second = jnp.where(core == 0, other, own)
            wide = jnp.concatenate([first, first, second, second, tail], axis=0).astype(BF16)
            for part in range(blocks):
                block = wide[:, part * LANES : (part + 1) * LANES].T
                table[pl.ds(start + part * LANES, LANES), :] = block.astype(F32)
            return carry

        lax.fori_loop(0, table_rows // span, turn, 0)
        table[pl.ds(table_rows, 8), :] = jnp.zeros((8, LANES), F32)

        unroll = 16
        chunks = owner_rows // unroll

        def look_up(step, carry):
            owner = step // chunks
            source = (owner * 2 + core) * owner_rows + (step % chunks) * unroll
            for part in range(unroll):
                terms = [
                    table[pl.ds(index_ref[slot * group_rows + source + part], 1), :] for slot in range(slots)
                ]
                while len(terms) > 1:
                    terms = [a + b for a, b in zip(terms[::2], terms[1::2])]
                self_row = table[pl.ds(target_ref[source + part], 1), :]
                mean_row = terms[0] / count_ref[source + part].astype(F32)
                rows[pl.ds(step * unroll + part, 1), :] = jnp.where(is_self, self_row, mean_row)
            return carry

        lax.fori_loop(0, owners * chunks, look_up, 0)

        fold = relative_ref.shape[1]
        for owner in range(owners):
            values = rows[pl.ds(owner * owner_rows, owner_rows), :].astype(BF16)
            out_ref[owner] = values[:, : 4 * slice_width]
            turn_y = lax.rem(owner % owners_y - here + owners_y, owners_y)
            for part in range(owner_rows // fold):
                column = (owner // owners_y * (owner_rows // fold) + part) * LANES
                relative_ref[turn_y, :, column : column + LANES] = values[part * fold : (part + 1) * fold]

    smem = pl.BlockSpec(memory_space=pltpu.SMEM)
    vmem = pl.BlockSpec(memory_space=pltpu.VMEM)
    return pl.pallas_call(
        kernel,
        out_shape=(
            jax.ShapeDtypeStruct((owners, owner_rows, 4 * slice_width), BF16),
            jax.ShapeDtypeStruct((owners_y, owners // owners_y * owner_rows * LANES // width, width), BF16),
        ),
        in_specs=[smem, smem, smem, smem, vmem, vmem],
        out_specs=(vmem, vmem),
        scratch_shapes=[
            pltpu.VMEM((table_rows + 8, LANES), F32),
            pltpu.VMEM((owners * owner_rows, LANES), F32),
        ],
        compiler_params=pltpu.CompilerParams(vmem_limit_bytes=30 << 20),
        cost_estimate=pl.CostEstimate(flops=50_000_000, bytes_accessed=100_000_000, transcendentals=0),
        name="gather_mean",
    )


def silu_slope(values):
    sig = jax.nn.sigmoid(values)
    return sig * (1.0 + values * (1.0 - sig))


def swap(values):
    return lax.ppermute(values, "core", [(0, 1), (1, 0)])


def exchange(values, axis):
    return lax.all_to_all(values, axis, split_axis=0, concat_axis=0, tiled=True)


def turn_blocks(blocks, axis):
    n = len(blocks)
    here = lax.axis_index(axis)
    got = [blocks[0]] + [lax.ppermute(blocks[k], axis, [(i, (i + k) % n) for i in range(n)]) for k in range(1, n)]
    return got, lambda got: jnp.stack(
        [lax.dynamic_index_in_dim(jnp.stack(got), (here - j) % n, 0, keepdims=False) for j in range(n)]
    )


def body(
    node_features,
    first_weight,
    second_weight,
    target_nodes,
    outer_nodes,
    outer_counts,
    inner_nodes,
    inner_counts,
    cotangent,
):
    nx, ny, nb = lax.axis_size("x"), lax.axis_size("y"), lax.axis_size("batch")
    core = lax.axis_index("core")
    slice_width, nodes = node_features.shape
    width = second_weight.shape[1]
    half = width // 2
    group_rows, slots = outer_nodes.shape[1:]
    owner_rows = group_rows // (nx * ny * 2)
    second_rows, fan_inner = inner_nodes.shape[1:]
    both = 2 * slice_width
    upstream = cotangent[0]

    weight = first_weight.transpose(1, 0, 2).reshape(both, width)
    weight_mine = exchange(jnp.broadcast_to(weight[None], (nx * ny,) + weight.shape), ("x", "y"))
    weight_mine = weight_mine.reshape(nx * ny * both, width)

    counts = outer_counts[0]
    live = jnp.arange(slots, dtype=jnp.int32)[:, None] < counts[None, :]
    index = jnp.where(live, outer_nodes[0].T, nodes).reshape(-1)
    other_features = swap(node_features)
    stacked, relative = gather_kernel(slots, nx * ny, ny, owner_rows, slice_width, nodes, width)(
        jnp.stack([core, lax.axis_index("y")]).astype(jnp.int32),
        index,
        target_nodes[0],
        counts,
        node_features,
        other_features,
    )
    stacked, weight_mine = lax.optimization_barrier((stacked, weight_mine))
    weight_other, late_upstream = lax.optimization_barrier((swap(weight_mine), upstream))
    owned = exchange(stacked, ("x", "y"))
    owned = owned.reshape(nx * ny, owner_rows, 2, both).transpose(2, 1, 0, 3).reshape(2, owner_rows, nx * ny * both)
    pre = jnp.dot(jnp.where(core == 0, owned[0], owned[1]), weight_mine, preferred_element_type=F32)
    pre += jnp.dot(jnp.where(core == 0, owned[1], owned[0]), weight_other, preferred_element_type=F32)
    hidden = jax.nn.silu(pre).astype(BF16)

    inner = inner_nodes[0]
    inner_cnt = inner_counts[0]
    inner_live = (jnp.arange(fan_inner, dtype=jnp.int32)[None, :] < inner_cnt[:, None]).astype(F32)
    columns = jnp.arange(owner_rows, dtype=jnp.int32)
    tally = jnp.sum((inner[:, :, None] == columns[None, None, :]).astype(F32) * inner_live[:, :, None], axis=1)
    divisor = inner_cnt.astype(F32)[:, None]
    mean_rows = (jnp.dot(tally.astype(BF16), hidden, preferred_element_type=F32) / divisor).astype(BF16)
    joined = jnp.concatenate([hidden[:second_rows], mean_rows], axis=1)
    output = jnp.dot(joined, second_weight, preferred_element_type=F32).astype(BF16)
    grad_joined = lax.dot_general(late_upstream, second_weight, (((1,), (1,)), ((), ())), preferred_element_type=F32)
    spread = lax.dot_general(
        tally, grad_joined[:, width:] / divisor, (((0,), (0,)), ((), ())), precision=lax.Precision.HIGHEST
    )
    grad_hidden = spread + jnp.pad(grad_joined[:, :width], ((0, owner_rows - second_rows), (0, 0)))
    grad_pre = (grad_hidden * silu_slope(pre)).astype(BF16)

    message = jnp.broadcast_to(grad_pre[None], (nx, owner_rows, width))
    columns_y = joined.reshape(second_rows, nx, ny, -1)
    here = lax.axis_index("y")
    folded = second_rows // 2
    pieces = []
    for k in range(ny):
        columns = lax.dynamic_index_in_dim(columns_y, (here + k) % ny, 2, keepdims=False).reshape(second_rows, -1)
        pieces.append(jnp.concatenate([columns[:folded], columns[folded:]], axis=1))
    packed = [jnp.concatenate([pieces[k], upstream, relative[k]], axis=0) for k in range(ny)]
    grad_pre_x = exchange(message, "x").reshape(nx * owner_rows, width)
    packed, in_order = turn_blocks(packed, "y")
    grad_pre_x, packed = lax.optimization_barrier((grad_pre_x, packed))
    along_y = in_order([block[folded + second_rows :] for block in packed])
    along_y = along_y.reshape(ny, -1, width // LANES, LANES).transpose(0, 2, 1, 3)
    along_y = along_y.reshape(ny, nx * owner_rows, LANES)[:, :, : 2 * both]
    packed = jnp.stack(packed)
    columns_y = packed[:, :folded]
    chunk = columns_y.shape[2] // 2
    columns_y = jnp.concatenate([columns_y[:, :, :chunk], columns_y[:, :, chunk:]], axis=1)
    columns_y = columns_y.reshape(ny * second_rows, chunk)
    upstream_y = packed[:, folded : folded + second_rows].reshape(ny * second_rows, width)
    first_terms = lax.dot_general(
        along_y, grad_pre_x, (((1,), (0,)), ((), ())), preferred_element_type=F32
    ).reshape(ny, 2, both, width)

    kept = lax.dynamic_index_in_dim(first_terms, core, 1, keepdims=False)
    sent = swap(lax.dynamic_index_in_dim(first_terms, 1 - core, 1, keepdims=False).astype(BF16))
    piece = width // nb
    first_terms = (kept + sent.astype(F32)).astype(BF16).reshape(ny, both, nb, piece).transpose(0, 2, 1, 3)
    first_terms = first_terms.reshape(ny * nb, both, piece)
    _, columns_y = lax.optimization_barrier((first_terms, columns_y))
    first_terms = exchange(first_terms, ("y", "batch"))
    first_piece = jnp.sum(first_terms.astype(F32), axis=0).astype(BF16)

    second_terms = lax.dot_general(
        columns_y, upstream_y, (((0,), (0,)), ((), ())), preferred_element_type=F32
    ).reshape(nx, 2, -1, width)
    kept = lax.dynamic_index_in_dim(second_terms, core, 1, keepdims=False)
    sent = swap(lax.dynamic_index_in_dim(second_terms, 1 - core, 1, keepdims=False).astype(BF16))
    second_terms = (kept + sent.astype(F32)).astype(BF16)
    here = lax.axis_index("x")
    got, _ = turn_blocks(
        [lax.dynamic_index_in_dim(second_terms, (here + k) % nx, 0, keepdims=False) for k in range(nx)], "x"
    )
    second_terms = sum(block.astype(F32) for block in got).astype(BF16)
    second_terms = second_terms.reshape(nb, -1, nb, piece).transpose(0, 2, 1, 3).reshape(nb, -1, piece)
    message = jnp.concatenate([jnp.broadcast_to(first_piece[None], (nb, both, piece)), second_terms], axis=1)
    message = exchange(message, "batch")
    grad_second = jnp.sum(message[:, both:].astype(F32), axis=0)
    grad_second = grad_second.reshape(nb, -1, piece).transpose(1, 0, 2).reshape(-1, width)
    grad_first = message[:, :both].reshape(nb, 2, slice_width, piece)
    grad_first = grad_first.transpose(2, 1, 0, 3).reshape(slice_width, 2, width)
    return (output[None], grad_second, grad_first.astype(F32))


def solution(mesh):
    feat, batch = mesh.devices.shape
    fine = Mesh(mesh.devices.reshape(4, feat // 8, 2, batch), ("x", "y", "core", "batch"))
    f = ("x", "y", "core")
    in_specs = (
        P(f, None),
        P(f, None, None),
        P(),
        P("batch", None),
        P("batch", None, None),
        P("batch", None),
        P("batch", f, None),
        P("batch", f),
        P("batch", f, None),
    )
    out_specs = (P("batch", f, None), P(("x", "y", "core", "batch"), None), P(f, None, None))
    return jax.shard_map(body, mesh=fine, in_specs=in_specs, out_specs=out_specs, check_vma=False)
```

time: 136 us -> 120 us (0.88); the launches traced: 134 us -> 119 us
  Pallas kernels: 33.1 us -> 21.4 us
  matrix products: 10.7 us -> 8.82 us
    pallas_call x1, Pallas kernels: 33.1 us -> 21.4 us  [body(): gather_kernel(slots, nx * ny, ny, owner_rows, slice_width, nodes, width)]
    dot_general x1, matrix products: 3.51 us -> 1.32 us  [body(): lax.dot_general(late_upstream, second_weight, (((1,), (1,)), ((), ())), p...]
    unnamed x24 -> x23, local copies, waits for them, and re-layouts: 3.07 us -> 3.1 us
  transfers between devices with their start and end apart: 16 -> 15, of which waited for: 11 -> 10; matrix products, arithmetic and copies ran while one was open for 9% -> 9% of each run, Pallas kernels for 25% -> 18%
where the time goes in v2:
time: 120 us; the launch traced here: 119 us
  starting transfers between devices  44.3 us (37%)
  waiting for transfers between devices  32.7 us (27%)
  Pallas kernels  21.4 us (18%)
  matrix products  8.82 us (7%)
  local copies, waits for them, and re-layouts  7.77 us (6%)
  other arithmetic  3.33 us (3%)
    all_to_all x5, starting transfers between devices, exchange(): return lax.all_to_all(values, axis, split_axis=0, concat_axis=0, tiled=True)  35.1 us
    pallas_call x1, Pallas kernels, body(): gather_kernel(slots, nx * ny, ny, owner_rows, slice_width, nodes, width)  21.4 us
    all_to_all x5, waiting for transfers between devices, exchange(): return lax.all_to_all(values, axis, split_axis=0, concat_axis=0, tiled=True)  16.7 us
    ppermute x6, waiting for transfers between devices, turn_blocks(): lax.ppermute(blocks[k], axis, [(i, (i + k) % n) for i in range(n)])  14.3 us
    ppermute x6, starting transfers between devices, turn_blocks(): lax.ppermute(blocks[k], axis, [(i, (i + k) % n) for i in range(n)])  8.82 us
    dot_general x1, matrix products, body(): jnp.dot(joined, second_weight, preferred_element_type=F32).astype(BF16)  3.65 us
    unnamed x23, local copies, waits for them, and re-layouts  3.1 us
  transfers between devices with their start and end apart: 15, of which 10 were waited for; matrix products, arithmetic and copies ran while one was open for 9% of the time, Pallas kernels for 18%

profile of v2, /device:TPU:8, one launch (start us, length us, event | category | flops | bytes accessed | tf_op | source)
XLA Modules:
  0.0 119.4 jit_solution(7440209545331907777)
XLA Ops:
  0.7 0.9 copy.47
  1.6 1.3 %broadcast_in_dim.16 = bf16[16,48,1024]{2,1,0:T(8,128)(2,1)} broadcast(bf16[48,1024]{1,0:T(8,128)(2,1)S(1)} %bitcast.179), dimensions={1,2} | broadcast | bytes 1671168 | tf_op jit(solution)/shard_map/broadcast_in_dim | solution.py:131
  3.0 7.5 %all-to-all-start = ((bf16[16,48,1024]{2,1,0:T(8,128)(2,1)}), bf16[16,48,1024]{2,1,0:T(8,128)(2,1)}, u32[]{:S(2)}, u32[]{:S(2)}) async-start(bf16[16,48,1024]{2,1,0:T(8,128)(2,1)} %broadcast_in_dim.16), calls=%async_computation | async-start | bytes 3145728 | tf_op jit(solution)/shard_map/all_to_all | solution.py:96
  10.7 21.4 %gather_mean.1 = (bf16[16,64,96]{2,1,0:T(8,128)(2,1)S(1)}, bf16[4,32,1024]{2,1,0:T(8,128)(2,1)S(1)}) custom-call(s32[2]{0:T(128)S(1)} %pad_add_fusion.place_ref, s32[32768]{0:T(1024)S(1)} %bitcast.155, s32[2048]{0:T(1024)S(1)} %bitcast.158, s32[2048]{0:T(1024)S(1)} %bitcast.157, bf16[24,32768]{1,0:T(8,128)(2,1)S(1)} %copy-done, ...), custom_call_target="tpu_custom_call" | custom-call | flops 50000000 | bytes 100000000 | tf_op jit(solution)/shard_map/gather_mean/pallas_call | solution.py:138
  32.8 1.7 %all-to-all-done = bf16[16,48,1024]{2,1,0:T(8,128)(2,1)} async-done(((bf16[16,48,1024]{2,1,0:T(8,128)(2,1)}), bf16[16,48,1024]{2,1,0:T(8,128)(2,1)}, u32[]{:S(2)}, u32[]{:S(2)}) %all-to-all-start) | async-done | bytes 1572896 | tf_op jit(solution)/shard_map/all_to_all | solution.py:96
  34.8 5.6 %all-to-all-start.1 = ((bf16[16,64,96]{2,1,0:T(8,128)(2,1)}), bf16[16,64,96]{2,1,0:T(8,128)(2,1)S(1)}, u32[]{:S(2)}, u32[]{:S(2)}) async-start(bf16[16,64,96]{2,1,0:T(8,128)(2,1)} %copy-done.1), calls=%async_computation.1 | async-start | bytes 524288 | tf_op jit(solution)/shard_map/all_to_all | solution.py:96
  40.4 7.6 %all-to-all-done.1 = bf16[16,64,96]{2,1,0:T(8,128)(2,1)S(1)} async-done(((bf16[16,64,96]{2,1,0:T(8,128)(2,1)}), bf16[16,64,96]{2,1,0:T(8,128)(2,1)S(1)}, u32[]{:S(2)}, u32[]{:S(2)}) %all-to-all-start.1) | async-done | bytes 196640 | tf_op jit(solution)/shard_map/all_to_all | solution.py:96
  48.3 2.0 %fusion.31 = f32[64,1024]{1,0:T(8,128)S(1)} fusion(bf16[64,768]{0,1:T(8,128)(2,1)S(1)} %bitcast.176, bf16[768,1024]{1,0:T(8,128)(2,1)} %bitcast.8), kind=kOutput, calls=%fused_computation.102 | convolution fusion | flops 100663296 | bytes 1933312 | tf_op jit(solution)/shard_map/dot_general | solution.py:150
  51.3 1.3 %fusion.32 = f32[32,2048]{1,0:T(8,128)S(1)} fusion(bf16[32,1024]{1,0:T(8,128)(2,1)S(1)} %bitcast.181, bf16[2048,1024]{1,0:T(8,128)(2,1)S(1)} %copy-done.4), kind=kOutput, calls=%fused_computation.103 | convolution fusion | flops 134217728 | bytes 4521984 | tf_op jit(solution)/shard_map/dot_general | solution.py:163
  53.3 0.9 broadcast_in_dim.18
  54.1 3.5 %all-to-all-start.2 = ((bf16[4,64,1024]{2,1,0:T(8,128)(2,1)}), bf16[4,64,1024]{2,1,0:T(8,128)(2,1)S(1)}, u32[]{:S(2)}, u32[]{:S(2)}) async-start(bf16[4,64,1024]{2,1,0:T(8,128)(2,1)} %broadcast_in_dim.18), calls=%async_computation.2 | async-start | bytes 1048576 | tf_op jit(solution)/shard_map/all_to_all | solution.py:96
  57.7 0.8 dynamic-slice_reduce_fusion.1
  58.7 1.1 collective-permute-start.2
  59.8 2.7 %collective-permute-start.3 = (bf16[80,1024]{1,0:T(8,128)(2,1)S(1)}, bf16[80,1024]{1,0:T(8,128)(2,1)S(1)}, u32[]{:S(2)}, u32[]{:S(2)}) collective-permute-start(bf16[80,1024]{1,0:T(8,128)(2,1)S(1)} %get-tuple-element.56), channel_id=1, source_target_pairs={{0,32},{16,48},{32,0},{48,16},{1,33},{17,49},{33,1},{49,17},{2,34}... | collective-permute-start | bytes 491528 | tf_op jit(solution)/shard_map/ppermute | solution.py:102
  62.8 3.0 %collective-permute-done.2 = bf16[80,1024]{1,0:T(8,128)(2,1)S(1)} collective-permute-done((bf16[80,1024]{1,0:T(8,128)(2,1)S(1)}, bf16[80,1024]{1,0:T(8,128)(2,1)S(1)}, u32[]{:S(2)}, u32[]{:S(2)}) %collective-permute-start.2) | collective-permute-done | bytes 163872 | tf_op jit(solution)/shard_map/ppermute | solution.py:102
  65.7 2.2 %collective-permute-done.3 = bf16[80,1024]{1,0:T(8,128)(2,1)S(1)} collective-permute-done((bf16[80,1024]{1,0:T(8,128)(2,1)S(1)}, bf16[80,1024]{1,0:T(8,128)(2,1)S(1)}, u32[]{:S(2)}, u32[]{:S(2)}) %collective-permute-start.3) | collective-permute-done | bytes 163872 | tf_op jit(solution)/shard_map/ppermute | solution.py:102
  68.0 1.7 %collective-permute-done.4 = bf16[80,1024]{1,0:T(8,128)(2,1)S(1)} collective-permute-done((bf16[80,1024]{1,0:T(8,128)(2,1)S(1)}, bf16[80,1024]{1,0:T(8,128)(2,1)S(1)}, u32[]{:S(2)}, u32[]{:S(2)}) %collective-permute-start.4) | collective-permute-done | bytes 163872 | tf_op jit(solution)/shard_map/ppermute | solution.py:102
  70.4 1.7 %collective-permute-done.5 = bf16[4,48,1024]{2,1,0:T(8,128)(2,1)S(1)} collective-permute-done((bf16[4,48,1024]{2,1,0:T(8,128)(2,1)S(1)}, bf16[4,48,1024]{2,1,0:T(8,128)(2,1)S(1)}, u32[]{:S(2)}, u32[]{:S(2)}) %collective-permute-start.5) | collective-permute-done | bytes 393248 | tf_op jit(solution)/shard_map/ppermute | solution.py:92
  72.3 0.8 copy.59
  74.0 11.8 %all-to-all-start.3 = ((bf16[32,48,128]{2,1,0:T(8,128)(2,1)}), bf16[32,48,128]{2,1,0:T(8,128)(2,1)S(1)}, u32[]{:S(2)}, u32[]{:S(2)}) async-start(bf16[32,48,128]{2,1,0:T(8,128)(2,1)} %bitcast.34), calls=%async_computation.3 | async-start | bytes 786432 | tf_op jit(solution)/shard_map/all_to_all | solution.py:96
  85.8 1.2 fusion.4
  87.1 3.0 %collective-permute-start.9 = (bf16[64,1024]{1,0:T(8,128)(2,1)S(1)}, bf16[64,1024]{1,0:T(8,128)(2,1)S(1)}, u32[]{:S(2)}, u32[]{:S(2)}) collective-permute-start(bf16[64,1024]{1,0:T(8,128)(2,1)S(1)} %get-tuple-element.42), channel_id=1, source_target_pairs={{0,192},{64,0},{128,64},{192,128},{1,193},{65,1},{129,65},{193,129... | collective-permute-start | bytes 393224 | tf_op jit(solution)/shard_map/ppermute | solution.py:102
  90.1 0.9 collective-permute-start.8
  90.9 0.9 collective-permute-start.7
  91.8 3.8 %collective-permute-done.9 = bf16[64,1024]{1,0:T(8,128)(2,1)S(1)} collective-permute-done((bf16[64,1024]{1,0:T(8,128)(2,1)S(1)}, bf16[64,1024]{1,0:T(8,128)(2,1)S(1)}, u32[]{:S(2)}, u32[]{:S(2)}) %collective-permute-start.9) | collective-permute-done | bytes 131104 | tf_op jit(solution)/shard_map/ppermute | solution.py:102
  95.6 2.3 %collective-permute-done.8 = bf16[64,1024]{1,0:T(8,128)(2,1)S(1)} collective-permute-done((bf16[64,1024]{1,0:T(8,128)(2,1)S(1)}, bf16[64,1024]{1,0:T(8,128)(2,1)S(1)}, u32[]{:S(2)}, u32[]{:S(2)}) %collective-permute-start.8) | collective-permute-done | bytes 131104 | tf_op jit(solution)/shard_map/ppermute | solution.py:102
  97.9 1.4 %collective-permute-done.7 = bf16[64,1024]{1,0:T(8,128)(2,1)S(1)} collective-permute-done((bf16[64,1024]{1,0:T(8,128)(2,1)S(1)}, bf16[64,1024]{1,0:T(8,128)(2,1)S(1)}, u32[]{:S(2)}, u32[]{:S(2)}) %collective-permute-start.7) | collective-permute-done | bytes 131104 | tf_op jit(solution)/shard_map/ppermute | solution.py:102
  99.5 0.7 pad_maximum_fusion.8
  100.2 6.6 %all-to-all-start.4 = ((bf16[8,112,128]{2,1,0:T(8,128)(2,1)}), bf16[8,112,128]{2,1,0:T(8,128)(2,1)S(1)}, u32[]{:S(2)}, u32[]{:S(2)}) async-start(bf16[8,112,128]{2,1,0:T(8,128)(2,1)} %pad_maximum_fusion.8), calls=%async_computation.4 | async-start | bytes 458752 | tf_op jit(solution)/shard_map/all_to_all | solution.py:96
  106.8 3.6 %fusion.3 = bf16[1,32,1024]{2,1,0:T(8,128)(2,1)} fusion(bf16[2048,1024]{1,0:T(8,128)(2,1)} %param.11, bf16[32,1024]{1,0:T(8,128)(2,1)S(1)} %fusion.2, bf16[32,1024]{1,0:T(8,128)(2,1)S(1)} %slice.149), kind=kOutput, calls=%fused_computation.7 | convolution fusion | flops 134512640 | bytes 4390912 | tf_op jit(solution)/shard_map/dot_general | solution.py:162
  110.5 7.4 %all-to-all-done.4 = bf16[8,112,128]{2,1,0:T(8,128)(2,1)S(1)} async-done(((bf16[8,112,128]{2,1,0:T(8,128)(2,1)}), bf16[8,112,128]{2,1,0:T(8,128)(2,1)S(1)}, u32[]{:S(2)}, u32[]{:S(2)}) %all-to-all-start.4) | async-done | bytes 229408 | tf_op jit(solution)/shard_map/all_to_all | solution.py:96
  118.0 0.8 reshape.146
  (75 shorter events, 6.3 us)
Async XLA Ops:
  0.6 10.1 %collective-permute-start = (bf16[24,32768]{1,0:T(8,128)(2,1)}, bf16[24,32768]{1,0:T(8,128)(2,1)S(1)}, u32[]{:S(2)}, u32[]{:S(2)}) collective-permute-start(bf16[24,32768]{1,0:T(8,128)(2,1)} %own_ref.1), channel_id=1, source_target_pairs={{0,8},{8,0},{1,9},{9,1},{2,10},{10,2},{3,11},{11,3},{4,12},{12,4},... | collective-permute-start | bytes 4718600 | tf_op jit(solution)/shard_map/ppermute | solution.py:92
  3.0 7.5 %copy-start.2 = (s32[1,2048]{1,0:T(1,128)S(1)}, s32[1,2048]{1,0:T(1,128)}, u32[]{:S(2)}) copy-start(s32[1,2048]{1,0:T(1,128)} %param.14) | copy-start | bytes 24580
  3.0 7.6 %copy-start.6 = (s32[1,2048,16]{1,2,0:T(8,128)S(1)}, s32[1,2048,16]{1,2,0:T(8,128)}, u32[]{:S(2)}) copy-start(s32[1,2048,16]{1,2,0:T(8,128)} %param.13) | copy-start | bytes 393220
  3.0 7.7 %copy-start = (bf16[24,32768]{1,0:T(8,128)(2,1)S(1)}, bf16[24,32768]{1,0:T(8,128)(2,1)}, u32[]{:S(2)}) copy-start(bf16[24,32768]{1,0:T(8,128)(2,1)} %own_ref.1) | copy-start | bytes 4718596
  3.0 7.7 %copy-start.3 = (s32[1,2048]{1,0:T(1,128)S(1)}, s32[1,2048]{1,0:T(1,128)}, u32[]{:S(2)}) copy-start(s32[1,2048]{1,0:T(1,128)} %param.12) | copy-start | bytes 24580
  3.0 31.5 %all-to-all-start = ((bf16[16,48,1024]{2,1,0:T(8,128)(2,1)}), bf16[16,48,1024]{2,1,0:T(8,128)(2,1)}, u32[]{:S(2)}, u32[]{:S(2)}) async-start(bf16[16,48,1024]{2,1,0:T(8,128)(2,1)} %broadcast_in_dim.16), calls=%async_computation | async-start | bytes 3145728 | tf_op jit(solution)/shard_map/all_to_all | solution.py:96
  10.7 23.8 %copy-start.7 = (s32[1,32,8]{1,2,0:T(8,128)S(1)}, s32[1,32,8]{1,2,0:T(8,128)}, u32[]{:S(2)}) copy-start(s32[1,32,8]{1,2,0:T(8,128)} %param.15) | copy-start | bytes 3076
  10.7 23.9 %copy-start.8 = (s32[1,32]{1,0:T(1,128)S(1)}, s32[1,32]{1,0:T(1,128)}, u32[]{:S(2)}) copy-start(s32[1,32]{1,0:T(1,128)} %param.16) | copy-start | bytes 388
  32.1 0.7 copy-start.1
  34.5 15.8 %collective-permute-start.1 = (bf16[768,1024]{1,0:T(8,128)(2,1)}, bf16[768,1024]{1,0:T(8,128)(2,1)S(1)}, u32[]{:S(2)}, u32[]{:S(2)}) collective-permute-start(bf16[768,1024]{1,0:T(8,128)(2,1)} %bitcast.8), channel_id=1, source_target_pairs={{0,8},{8,0},{1,9},{9,1},{2,10},{10,2},{3,11},{11,3},{4,12},{12,4},... | collective-permute-start | bytes 4718600 | tf_op jit(solution)/shard_map/ppermute | solution.py:92
  34.8 13.2 %all-to-all-start.1 = ((bf16[16,64,96]{2,1,0:T(8,128)(2,1)}), bf16[16,64,96]{2,1,0:T(8,128)(2,1)S(1)}, u32[]{:S(2)}, u32[]{:S(2)}) async-start(bf16[16,64,96]{2,1,0:T(8,128)(2,1)} %copy-done.1), calls=%async_computation.1 | async-start | bytes 524288 | tf_op jit(solution)/shard_map/all_to_all | solution.py:96
  48.3 2.7 %copy-start.4 = (bf16[2048,1024]{1,0:T(8,128)(2,1)S(1)}, bf16[2048,1024]{1,0:T(8,128)(2,1)}, u32[]{:S(2)}) copy-start(bf16[2048,1024]{1,0:T(8,128)(2,1)} %param.11) | copy-start | bytes 12582916
  50.3 1.0 copy-start.5
  54.1 15.5 %all-to-all-start.2 = ((bf16[4,64,1024]{2,1,0:T(8,128)(2,1)}), bf16[4,64,1024]{2,1,0:T(8,128)(2,1)S(1)}, u32[]{:S(2)}, u32[]{:S(2)}) async-start(bf16[4,64,1024]{2,1,0:T(8,128)(2,1)} %broadcast_in_dim.18), calls=%async_computation.2 | async-start | bytes 1048576 | tf_op jit(solution)/shard_map/all_to_all | solution.py:96
  58.7 7.1 %collective-permute-start.2 = (bf16[80,1024]{1,0:T(8,128)(2,1)S(1)}, bf16[80,1024]{1,0:T(8,128)(2,1)S(1)}, u32[]{:S(2)}, u32[]{:S(2)}) collective-permute-start(bf16[80,1024]{1,0:T(8,128)(2,1)S(1)} %get-tuple-element.55), channel_id=1, source_target_pairs={{0,16},{16,32},{32,48},{48,0},{1,17},{17,33},{33,49},{49,1},{2,18}... | collective-permute-start | bytes 491528 | tf_op jit(solution)/shard_map/ppermute | solution.py:102
  59.8 8.2 %collective-permute-start.3 = (bf16[80,1024]{1,0:T(8,128)(2,1)S(1)}, bf16[80,1024]{1,0:T(8,128)(2,1)S(1)}, u32[]{:S(2)}, u32[]{:S(2)}) collective-permute-start(bf16[80,1024]{1,0:T(8,128)(2,1)S(1)} %get-tuple-element.56), channel_id=1, source_target_pairs={{0,32},{16,48},{32,0},{48,16},{1,33},{17,49},{33,1},{49,17},{2,34}... | collective-permute-start | bytes 491528 | tf_op jit(solution)/shard_map/ppermute | solution.py:102
  62.5 7.1 %collective-permute-start.4 = (bf16[80,1024]{1,0:T(8,128)(2,1)S(1)}, bf16[80,1024]{1,0:T(8,128)(2,1)S(1)}, u32[]{:S(2)}, u32[]{:S(2)}) collective-permute-start(bf16[80,1024]{1,0:T(8,128)(2,1)S(1)} %get-tuple-element.54), channel_id=1, source_target_pairs={{0,48},{16,0},{32,16},{48,32},{1,49},{17,1},{33,17},{49,33},{2,50}... | collective-permute-start | bytes 491528 | tf_op jit(solution)/shard_map/ppermute | solution.py:102
  70.3 1.8 %collective-permute-start.5 = (bf16[4,48,1024]{2,1,0:T(8,128)(2,1)S(1)}, bf16[4,48,1024]{2,1,0:T(8,128)(2,1)S(1)}, u32[]{:S(2)}, u32[]{:S(2)}) collective-permute-start(bf16[4,48,1024]{2,1,0:T(8,128)(2,1)S(1)} %fusion.9), channel_id=1, source_target_pairs={{0,8},{8,0},{1,9},{9,1},{2,10},{10,2},{3,11},{11,3},{4,12},{12,4},... | collective-permute-start | bytes 1179656 | tf_op jit(solution)/shard_map/ppermute | solution.py:92
  73.7 12.1 %collective-permute-start.6 = (bf16[4,64,1024]{2,1,0:T(8,128)(2,1)S(1)}, bf16[4,64,1024]{2,1,0:T(8,128)(2,1)}, u32[]{:S(2)}, u32[]{:S(2)}) collective-permute-start(bf16[4,64,1024]{2,1,0:T(8,128)(2,1)S(1)} %fusion.6), channel_id=1, source_target_pairs={{0,8},{8,0},{1,9},{9,1},{2,10},{10,2},{3,11},{11,3},{4,12},{12,4},... | collective-permute-start | bytes 1572872 | tf_op jit(solution)/shard_map/ppermute | solution.py:92
  74.0 25.4 %all-to-all-start.3 = ((bf16[32,48,128]{2,1,0:T(8,128)(2,1)}), bf16[32,48,128]{2,1,0:T(8,128)(2,1)S(1)}, u32[]{:S(2)}, u32[]{:S(2)}) async-start(bf16[32,48,128]{2,1,0:T(8,128)(2,1)} %bitcast.34), calls=%async_computation.3 | async-start | bytes 786432 | tf_op jit(solution)/shard_map/all_to_all | solution.py:96
  87.1 8.5 %collective-permute-start.9 = (bf16[64,1024]{1,0:T(8,128)(2,1)S(1)}, bf16[64,1024]{1,0:T(8,128)(2,1)S(1)}, u32[]{:S(2)}, u32[]{:S(2)}) collective-permute-start(bf16[64,1024]{1,0:T(8,128)(2,1)S(1)} %get-tuple-element.42), channel_id=1, source_target_pairs={{0,192},{64,0},{128,64},{192,128},{1,193},{65,1},{129,65},{193,129... | collective-permute-start | bytes 393224 | tf_op jit(solution)/shard_map/ppermute | solution.py:102
  90.1 7.8 %collective-permute-start.8 = (bf16[64,1024]{1,0:T(8,128)(2,1)S(1)}, bf16[64,1024]{1,0:T(8,128)(2,1)S(1)}, u32[]{:S(2)}, u32[]{:S(2)}) collective-permute-start(bf16[64,1024]{1,0:T(8,128)(2,1)S(1)} %get-tuple-element.43), channel_id=1, source_target_pairs={{0,128},{64,192},{128,0},{192,64},{1,129},{65,193},{129,1},{193,65... | collective-permute-start | bytes 393224 | tf_op jit(solution)/shard_map/ppermute | solution.py:102
  90.9 8.4 %collective-permute-start.7 = (bf16[64,1024]{1,0:T(8,128)(2,1)S(1)}, bf16[64,1024]{1,0:T(8,128)(2,1)S(1)}, u32[]{:S(2)}, u32[]{:S(2)}) collective-permute-start(bf16[64,1024]{1,0:T(8,128)(2,1)S(1)} %get-tuple-element.41), channel_id=1, source_target_pairs={{0,64},{64,128},{128,192},{192,0},{1,65},{65,129},{129,193},{193,1... | collective-permute-start | bytes 393224 | tf_op jit(solution)/shard_map/ppermute | solution.py:102
  100.2 17.7 %all-to-all-start.4 = ((bf16[8,112,128]{2,1,0:T(8,128)(2,1)}), bf16[8,112,128]{2,1,0:T(8,128)(2,1)S(1)}, u32[]{:S(2)}, u32[]{:S(2)}) async-start(bf16[8,112,128]{2,1,0:T(8,128)(2,1)} %pad_maximum_fusion.8), calls=%async_computation.4 | async-start | bytes 458752 | tf_op jit(solution)/shard_map/all_to_all | solution.py:96

commit v3 on v2

--- a/solution.py
+++ b/solution.py
@@ -83,9 +83,72 @@
     )
 
 
-def silu_slope(values):
-    sig = jax.nn.sigmoid(values)
-    return sig * (1.0 + values * (1.0 - sig))
+def owner_kernel(nx, ny, owner_rows, second_rows, fan, width, both):
+    def kernel(place_ref, owned_ref, mine_ref, other_ref, inner_ref, count_ref, grad_ref,
+               message_ref, joined_ref, columns_ref):
+        core, here = place_ref[0], place_ref[1]
+        pre = jnp.zeros((owner_rows, width), F32)
+        for pair in range(nx * ny):
+            rows = owned_ref[pair]
+            turned = jnp.concatenate([rows[:, both:], rows[:, :both]], axis=1)
+            rows = jnp.where(core == 0, rows, turned)
+            weight = jnp.concatenate([mine_ref[pair], other_ref[pair]], axis=0)
+            pre += jnp.dot(rows, weight, preferred_element_type=F32)
+        sig = jax.nn.sigmoid(pre)
+        hidden = (pre * sig).astype(BF16)
+
+        count = count_ref[...]
+        row = lax.broadcasted_iota(jnp.int32, (owner_rows, second_rows), 0)
+        tally = jnp.zeros((owner_rows, second_rows), F32)
+        for slot in range(fan):
+            tally += jnp.where(inner_ref[slot : slot + 1, :] == row, 1.0, 0.0)
+        tally = tally.astype(BF16)
+        diagonal = lax.broadcasted_iota(jnp.int32, (second_rows, second_rows), 0) == lax.broadcasted_iota(
+            jnp.int32, (second_rows, second_rows), 1
+        )
+        divisor = jnp.sum(jnp.where(diagonal, count.astype(F32), 0.0), axis=1, keepdims=True)
+        rows_of = (((0,), (0,)), ((), ()))
+        mean_rows = lax.dot_general(tally, hidden, rows_of, preferred_element_type=F32) / divisor
+        joined_ref[:, :width] = hidden[:second_rows]
+        joined_ref[:, width:] = mean_rows.astype(BF16)
+
+        grad_self, grad_mean = grad_ref[:, :width], grad_ref[:, width:]
+        rest = grad_mean / divisor
+        grad_hidden = jnp.zeros((owner_rows, width), F32)
+        for _ in range(3):
+            part = rest.astype(BF16)
+            rest = rest - part.astype(F32)
+            grad_hidden += jnp.dot(tally, part, preferred_element_type=F32)
+        grad_hidden = jnp.concatenate(
+            [grad_hidden[:second_rows] + grad_self, grad_hidden[second_rows:]], axis=0
+        )
+        grad_pre = (grad_hidden * (sig * (1.0 + pre * (1.0 - sig)))).astype(BF16)
+        for x in range(nx):
+            message_ref[x] = grad_pre
+
+        half = second_rows // 2
+        for turn in range(ny):
+            y = lax.rem(here + turn, ny)
+            for x in range(nx):
+                columns = joined_ref[:, pl.ds(pl.multiple_of((x * ny + y) * LANES, LANES), LANES)]
+                columns_ref[turn, :, x * LANES : (x + 1) * LANES] = columns[:half]
+                columns_ref[turn, :, (nx + x) * LANES : (nx + x + 1) * LANES] = columns[half:]
+
+    smem = pl.BlockSpec(memory_space=pltpu.SMEM)
+    vmem = pl.BlockSpec(memory_space=pltpu.VMEM)
+    return pl.pallas_call(
+        kernel,
+        out_shape=(
+            jax.ShapeDtypeStruct((nx, owner_rows, width), BF16),
+            jax.ShapeDtypeStruct((second_rows, 2 * width), BF16),
+            jax.ShapeDtypeStruct((ny, second_rows // 2, 2 * nx * LANES), BF16),
+        ),
+        in_specs=[smem] + [vmem] * 6,
+        out_specs=(vmem, vmem, vmem),
+        compiler_params=pltpu.CompilerParams(vmem_limit_bytes=24 << 20),
+        cost_estimate=pl.CostEstimate(flops=350_000_000, bytes_accessed=9_000_000, transcendentals=65536),
+        name="owner_layers",
+    )
 
 
 def swap(values):
@@ -118,6 +181,7 @@
 ):
     nx, ny, nb = lax.axis_size("x"), lax.axis_size("y"), lax.axis_size("batch")
     core = lax.axis_index("core")
+    place = jnp.stack([core, lax.axis_index("y")]).astype(jnp.int32)
     slice_width, nodes = node_features.shape
     width = second_weight.shape[1]
     half = width // 2
@@ -129,14 +193,13 @@
 
     weight = first_weight.transpose(1, 0, 2).reshape(both, width)
     weight_mine = exchange(jnp.broadcast_to(weight[None], (nx * ny,) + weight.shape), ("x", "y"))
-    weight_mine = weight_mine.reshape(nx * ny * both, width)
 
     counts = outer_counts[0]
     live = jnp.arange(slots, dtype=jnp.int32)[:, None] < counts[None, :]
     index = jnp.where(live, outer_nodes[0].T, nodes).reshape(-1)
     other_features = swap(node_features)
     stacked, relative = gather_kernel(slots, nx * ny, ny, owner_rows, slice_width, nodes, width)(
-        jnp.stack([core, lax.axis_index("y")]).astype(jnp.int32),
+        place,
         index,
         target_nodes[0],
         counts,
@@ -144,37 +207,18 @@
         other_features,
     )
     stacked, weight_mine = lax.optimization_barrier((stacked, weight_mine))
-    weight_other, late_upstream = lax.optimization_barrier((swap(weight_mine), upstream))
+    weight_other = swap(weight_mine)
+    _, late_upstream, inner, inner_count = lax.optimization_barrier(
+        (relative, upstream, inner_nodes[0].T, inner_counts)
+    )
+    grad_joined = lax.dot_general(late_upstream, second_weight, (((1,), (1,)), ((), ())), preferred_element_type=F32)
+    inner = jnp.where(jnp.arange(fan_inner, dtype=jnp.int32)[:, None] < inner_count, inner, owner_rows)
     owned = exchange(stacked, ("x", "y"))
-    owned = owned.reshape(nx * ny, owner_rows, 2, both).transpose(2, 1, 0, 3).reshape(2, owner_rows, nx * ny * both)
-    pre = jnp.dot(jnp.where(core == 0, owned[0], owned[1]), weight_mine, preferred_element_type=F32)
-    pre += jnp.dot(jnp.where(core == 0, owned[1], owned[0]), weight_other, preferred_element_type=F32)
-    hidden = jax.nn.silu(pre).astype(BF16)
-
-    inner = inner_nodes[0]
-    inner_cnt = inner_counts[0]
-    inner_live = (jnp.arange(fan_inner, dtype=jnp.int32)[None, :] < inner_cnt[:, None]).astype(F32)
-    columns = jnp.arange(owner_rows, dtype=jnp.int32)
-    tally = jnp.sum((inner[:, :, None] == columns[None, None, :]).astype(F32) * inner_live[:, :, None], axis=1)
-    divisor = inner_cnt.astype(F32)[:, None]
-    mean_rows = (jnp.dot(tally.astype(BF16), hidden, preferred_element_type=F32) / divisor).astype(BF16)
-    joined = jnp.concatenate([hidden[:second_rows], mean_rows], axis=1)
+    message, joined, pieces = owner_kernel(nx, ny, owner_rows, second_rows, fan_inner, width, both)(
+        place, owned, weight_mine, weight_other, inner, inner_counts, grad_joined
+    )
     output = jnp.dot(joined, second_weight, preferred_element_type=F32).astype(BF16)
-    grad_joined = lax.dot_general(late_upstream, second_weight, (((1,), (1,)), ((), ())), preferred_element_type=F32)
-    spread = lax.dot_general(
-        tally, grad_joined[:, width:] / divisor, (((0,), (0,)), ((), ())), precision=lax.Precision.HIGHEST
-    )
-    grad_hidden = spread + jnp.pad(grad_joined[:, :width], ((0, owner_rows - second_rows), (0, 0)))
-    grad_pre = (grad_hidden * silu_slope(pre)).astype(BF16)
-
-    message = jnp.broadcast_to(grad_pre[None], (nx, owner_rows, width))
-    columns_y = joined.reshape(second_rows, nx, ny, -1)
-    here = lax.axis_index("y")
     folded = second_rows // 2
-    pieces = []
-    for k in range(ny):
-        columns = lax.dynamic_index_in_dim(columns_y, (here + k) % ny, 2, keepdims=False).reshape(second_rows, -1)
-        pieces.append(jnp.concatenate([columns[:folded], columns[folded:]], axis=1))
     packed = [jnp.concatenate([pieces[k], upstream, relative[k]], axis=0) for k in range(ny)]
     grad_pre_x = exchange(message, "x").reshape(nx * owner_rows, width)
     packed, in_order = turn_blocks(packed, "y")

time: 120 us -> 117 us (0.975); the launches traced: 119 us -> 115 us
  waiting for transfers between devices: 32.7 us -> 26.6 us
  Pallas kernels: 21.4 us -> 24.2 us
    all_to_all x5, waiting for transfers between devices: 16.7 us -> 13.4 us  [exchange(): return lax.all_to_all(values, axis, split_axis=0, concat_axis=0, tiled=True)]
    dot_general x4 -> x0, matrix products: 3.03 us -> none  [the longest x1 1.97 us: body(): jnp.dot(jnp.where(core == 0, owned[0], owned[1]), weight_mine, preferred_...]
    ppermute x6, waiting for transfers between devices: 14.3 us -> 11.5 us  [turn_blocks(): lax.ppermute(blocks[k], axis, [(i, (i + k) % n) for i in range(n)])]
    dot_general x1, matrix products: 1.32 us -> 3.54 us  [body(): lax.dot_general(late_upstream, second_weight, (((1,), (1,)), ((), ())), p...]
    pallas_call x0 -> x1, Pallas kernels: none -> 2.04 us  [body(): owner_kernel(nx, ny, owner_rows, second_rows, fan_inner, width, both)]
    all_to_all x5, starting transfers between devices: 35.1 us -> 33.6 us  [exchange(): return lax.all_to_all(values, axis, split_axis=0, concat_axis=0, tiled=True)]
  transfers between devices with their start and end apart: 15 -> 15, of which waited for: 10 -> 10; matrix products, arithmetic and copies ran while one was open for 9% -> 12% of each run, Pallas kernels for 18% -> 19%
where the time goes in v3:
time: 117 us; the launch traced here: 115 us
  starting transfers between devices  43.9 us (38%)
  waiting for transfers between devices  26.6 us (23%)
  Pallas kernels  24.2 us (21%)
  matrix products  8.01 us (7%)
  local copies, waits for them, and re-layouts  7.4 us (6%)
  other arithmetic  4.04 us (3%)
    all_to_all x5, starting transfers between devices, exchange(): return lax.all_to_all(values, axis, split_axis=0, concat_axis=0, tiled=True)  33.6 us
    pallas_call x1, Pallas kernels, body(): gather_kernel(slots, nx * ny, ny, owner_rows, slice_width, nodes, width)  22.2 us
    all_to_all x5, waiting for transfers between devices, exchange(): return lax.all_to_all(values, axis, split_axis=0, concat_axis=0, tiled=True)  13.4 us
    ppermute x6, waiting for transfers between devices, turn_blocks(): lax.ppermute(blocks[k], axis, [(i, (i + k) % n) for i in range(n)])  11.5 us
    ppermute x6, starting transfers between devices, turn_blocks(): lax.ppermute(blocks[k], axis, [(i, (i + k) % n) for i in range(n)])  9.92 us
    dot_general x1, matrix products, body(): jnp.dot(joined, second_weight, preferred_element_type=F32).astype(BF16)  3.65 us
    dot_general x1, matrix products, body(): lax.dot_general(late_upstream, second_weight, (((1,), (1,)), ((), ())), p...  3.54 us
    unnamed x23, local copies, waits for them, and re-layouts  3.34 us
  transfers between devices with their start and end apart: 15, of which 10 were waited for; matrix products, arithmetic and copies ran while one was open for 12% of the time, Pallas kernels for 19%

profile of v3, /device:TPU:8, one launch (start us, length us, event | category | flops | bytes accessed | tf_op | source)
XLA Modules:
  0.0 115.1 jit_solution(17382104696919003782)
XLA Ops:
  0.7 0.9 copy.18
  1.7 1.3 %broadcast_in_dim.28 = bf16[16,48,1024]{2,1,0:T(8,128)(2,1)} broadcast(bf16[48,1024]{1,0:T(8,128)(2,1)S(1)} %bitcast.151), dimensions={1,2} | broadcast | bytes 1671168 | tf_op jit(solution)/shard_map/broadcast_in_dim | solution.py:195
  3.0 7.5 %all-to-all-start = ((bf16[16,48,1024]{2,1,0:T(8,128)(2,1)}), bf16[16,48,1024]{2,1,0:T(8,128)(2,1)S(1)}, u32[]{:S(2)}, u32[]{:S(2)}) async-start(bf16[16,48,1024]{2,1,0:T(8,128)(2,1)} %broadcast_in_dim.28), calls=%async_computation | async-start | bytes 3145728 | tf_op jit(solution)/shard_map/all_to_all | solution.py:159
  10.7 22.2 %gather_mean.1 = (bf16[16,64,96]{2,1,0:T(8,128)(2,1)}, bf16[4,32,1024]{2,1,0:T(8,128)(2,1)S(1)}) custom-call(s32[2]{0:T(128)S(1)} %pad_add_fusion.place_ref, s32[32768]{0:T(1024)S(1)} %bitcast.129, s32[2048]{0:T(1024)S(1)} %bitcast.132, s32[2048]{0:T(1024)S(1)} %bitcast.131, bf16[24,32768]{1,0:T(8,128)(2,1)S(1)} %copy-done, ...), custom_call_target="tpu_custom_call" | custom-call | flops 50000000 | bytes 100000000 | tf_op jit(solution)/shard_map/gather_mean/pallas_call | solution.py:201
  32.9 1.5 %all-to-all-done.mine_ref = bf16[16,48,1024]{2,1,0:T(8,128)(2,1)S(1)} async-done(((bf16[16,48,1024]{2,1,0:T(8,128)(2,1)}), bf16[16,48,1024]{2,1,0:T(8,128)(2,1)S(1)}, u32[]{:S(2)}, u32[]{:S(2)}) %all-to-all-start) | async-done | bytes 1572896 | tf_op jit(solution)/shard_map/all_to_all | solution.py:159
  34.4 5.7 %all-to-all-start.1 = ((bf16[16,64,96]{2,1,0:T(8,128)(2,1)}), bf16[16,64,96]{2,1,0:T(8,128)(2,1)}, u32[]{:S(2)}, u32[]{:S(2)}) async-start(bf16[16,64,96]{2,1,0:T(8,128)(2,1)} %get-tuple-element.20), calls=%async_computation.1 | async-start | bytes 524288 | tf_op jit(solution)/shard_map/all_to_all | solution.py:159
  40.8 3.5 %fusion.26.grad_ref = f32[32,2048]{1,0:T(8,128)S(1)} fusion(bf16[32,1024]{1,0:T(8,128)(2,1)S(1)} %bitcast.154, bf16[2048,1024]{1,0:T(8,128)(2,1)} %param.11), kind=kOutput, calls=%fused_computation.73 | convolution fusion | flops 134217728 | bytes 4521984 | tf_op jit(solution)/shard_map/dot_general | solution.py:214
  44.4 3.6 %all-to-all-done.1.owned_ref = bf16[16,64,96]{2,1,0:T(8,128)(2,1)} async-done(((bf16[16,64,96]{2,1,0:T(8,128)(2,1)}), bf16[16,64,96]{2,1,0:T(8,128)(2,1)}, u32[]{:S(2)}, u32[]{:S(2)}) %all-to-all-start.1) | async-done | bytes 196640 | tf_op jit(solution)/shard_map/all_to_all | solution.py:159
  48.0 2.0 %owner_layers.1 = (bf16[4,64,1024]{2,1,0:T(8,128)(2,1)S(1)}, bf16[32,2048]{1,0:T(8,128)(2,1)S(1)}, bf16[4,16,1024]{2,1,0:T(8,128)(2,1)S(1)}) custom-call(s32[2]{0:T(128)S(1)} %pad_add_fusion.place_ref, bf16[16,64,96]{2,1,0:T(8,128)(2,1)} %all-to-all-done.1.owned_ref, bf16[16,48,1024]{2,1,0:T(8,128)(2,1)S(1)} %all-to-all-done.mine_ref, ...), custom_call_target="tpu_custom_call" | custom-call | flops 350000000 | bytes 9000000 | tf_op jit(solution)/shard_map/owner_layers/pallas_call | solution.py:217
  50.1 0.8 copy-done.1
  51.5 3.5 %all-to-all-start.2 = ((bf16[4,64,1024]{2,1,0:T(8,128)(2,1)}), bf16[4,64,1024]{2,1,0:T(8,128)(2,1)S(1)}, u32[]{:S(2)}, u32[]{:S(2)}) async-start(bf16[4,64,1024]{2,1,0:T(8,128)(2,1)} %copy-done.1), calls=%async_computation.2 | async-start | bytes 1048576 | tf_op jit(solution)/shard_map/all_to_all | solution.py:159
  55.0 0.8 slice_bitcast_fusion.8
  55.8 1.0 fusion.18
  56.9 1.1 collective-permute-start.2
  57.9 2.7 %collective-permute-start.3 = (bf16[80,1024]{1,0:T(8,128)(2,1)S(1)}, bf16[80,1024]{1,0:T(8,128)(2,1)S(1)}, u32[]{:S(2)}, u32[]{:S(2)}) collective-permute-start(bf16[80,1024]{1,0:T(8,128)(2,1)S(1)} %get-tuple-element.55), channel_id=1, source_target_pairs={{0,32},{16,48},{32,0},{48,16},{1,33},{17,49},{33,1},{49,17},{2,34}... | collective-permute-start | bytes 491528 | tf_op jit(solution)/shard_map/ppermute | solution.py:165
  60.9 3.1 %collective-permute-done.2 = bf16[80,1024]{1,0:T(8,128)(2,1)S(1)} collective-permute-done((bf16[80,1024]{1,0:T(8,128)(2,1)S(1)}, bf16[80,1024]{1,0:T(8,128)(2,1)S(1)}, u32[]{:S(2)}, u32[]{:S(2)}) %collective-permute-start.2) | collective-permute-done | bytes 163872 | tf_op jit(solution)/shard_map/ppermute | solution.py:165
  64.0 2.1 %collective-permute-done.3 = bf16[80,1024]{1,0:T(8,128)(2,1)S(1)} collective-permute-done((bf16[80,1024]{1,0:T(8,128)(2,1)S(1)}, bf16[80,1024]{1,0:T(8,128)(2,1)S(1)}, u32[]{:S(2)}, u32[]{:S(2)}) %collective-permute-start.3) | collective-permute-done | bytes 163872 | tf_op jit(solution)/shard_map/ppermute | solution.py:165
  66.1 1.7 %collective-permute-done.4 = bf16[80,1024]{1,0:T(8,128)(2,1)S(1)} collective-permute-done((bf16[80,1024]{1,0:T(8,128)(2,1)S(1)}, bf16[80,1024]{1,0:T(8,128)(2,1)S(1)}, u32[]{:S(2)}, u32[]{:S(2)}) %collective-permute-start.4) | collective-permute-done | bytes 163872 | tf_op jit(solution)/shard_map/ppermute | solution.py:165
  68.6 1.7 %collective-permute-done.5 = bf16[4,48,1024]{2,1,0:T(8,128)(2,1)S(1)} collective-permute-done((bf16[4,48,1024]{2,1,0:T(8,128)(2,1)S(1)}, bf16[4,48,1024]{2,1,0:T(8,128)(2,1)S(1)}, u32[]{:S(2)}, u32[]{:S(2)}) %collective-permute-start.5) | collective-permute-done | bytes 393248 | tf_op jit(solution)/shard_map/ppermute | solution.py:155
  70.5 0.8 copy.22
  72.2 11.9 %all-to-all-start.3 = ((bf16[32,48,128]{2,1,0:T(8,128)(2,1)}), bf16[32,48,128]{2,1,0:T(8,128)(2,1)S(1)}, u32[]{:S(2)}, u32[]{:S(2)}) async-start(bf16[32,48,128]{2,1,0:T(8,128)(2,1)} %bitcast.33), calls=%async_computation.3 | async-start | bytes 786432 | tf_op jit(solution)/shard_map/all_to_all | solution.py:159
  84.1 1.2 %fusion.1 = bf16[4,64,1024]{2,1,0:T(8,128)(2,1)S(1)} fusion(bf16[4,64,1024]{2,1,0:T(8,128)(2,1)} %collective-permute-done.6, f32[4,2,64,1024]{3,2,1,0:T(8,128)S(1)} %fusion.27, s32[]{:T(128)S(6)} %select_n.89), kind=kLoop, calls=%fused_computation.3 | loop fusion | flops 786432 | bytes 2097156 | tf_op jit(solution)/shard_map/convert_element_type | solution.py:253
  85.3 1.8 %collective-permute-start.7 = (bf16[64,1024]{1,0:T(8,128)(2,1)S(1)}, bf16[64,1024]{1,0:T(8,128)(2,1)S(1)}, u32[]{:S(2)}, u32[]{:S(2)}) collective-permute-start(bf16[64,1024]{1,0:T(8,128)(2,1)S(1)} %get-tuple-element.38), channel_id=1, source_target_pairs={{0,64},{64,128},{128,192},{192,0},{1,65},{65,129},{129,193},{193,1... | collective-permute-start | bytes 393224 | tf_op jit(solution)/shard_map/ppermute | solution.py:165
  87.1 2.7 %collective-permute-start.8 = (bf16[64,1024]{1,0:T(8,128)(2,1)S(1)}, bf16[64,1024]{1,0:T(8,128)(2,1)S(1)}, u32[]{:S(2)}, u32[]{:S(2)}) collective-permute-start(bf16[64,1024]{1,0:T(8,128)(2,1)S(1)} %get-tuple-element.40), channel_id=1, source_target_pairs={{0,128},{64,192},{128,0},{192,64},{1,129},{65,193},{129,1},{193,65... | collective-permute-start | bytes 393224 | tf_op jit(solution)/shard_map/ppermute | solution.py:165
  89.8 1.5 %collective-permute-start.9 = (bf16[64,1024]{1,0:T(8,128)(2,1)S(1)}, bf16[64,1024]{1,0:T(8,128)(2,1)S(1)}, u32[]{:S(2)}, u32[]{:S(2)}) collective-permute-start(bf16[64,1024]{1,0:T(8,128)(2,1)S(1)} %get-tuple-element.39), channel_id=1, source_target_pairs={{0,192},{64,0},{128,64},{192,128},{1,193},{65,1},{129,65},{193,129... | collective-permute-start | bytes 393224 | tf_op jit(solution)/shard_map/ppermute | solution.py:165
  91.9 3.9 %collective-permute-done.8 = bf16[64,1024]{1,0:T(8,128)(2,1)S(1)} collective-permute-done((bf16[64,1024]{1,0:T(8,128)(2,1)S(1)}, bf16[64,1024]{1,0:T(8,128)(2,1)S(1)}, u32[]{:S(2)}, u32[]{:S(2)}) %collective-permute-start.8) | collective-permute-done | bytes 131104 | tf_op jit(solution)/shard_map/ppermute | solution.py:165
  95.8 1.7 %all-to-all-done.3 = bf16[32,48,128]{2,1,0:T(8,128)(2,1)S(1)} async-done(((bf16[32,48,128]{2,1,0:T(8,128)(2,1)}), bf16[32,48,128]{2,1,0:T(8,128)(2,1)S(1)}, u32[]{:S(2)}, u32[]{:S(2)}) %all-to-all-start.3) | async-done | bytes 393248 | tf_op jit(solution)/shard_map/all_to_all | solution.py:159
  97.6 0.7 pad_maximum_fusion.8
  98.3 5.0 %all-to-all-start.4 = ((bf16[8,112,128]{2,1,0:T(8,128)(2,1)}), bf16[8,112,128]{2,1,0:T(8,128)(2,1)S(1)}, u32[]{:S(2)}, u32[]{:S(2)}) async-start(bf16[8,112,128]{2,1,0:T(8,128)(2,1)} %pad_maximum_fusion.8), calls=%async_computation.4 | async-start | bytes 458752 | tf_op jit(solution)/shard_map/all_to_all | solution.py:159
  103.3 3.6 %fusion = bf16[1,32,1024]{2,1,0:T(8,128)(2,1)} fusion(bf16[32,2048]{1,0:T(8,128)(2,1)S(1)} %get-tuple-element.26, bf16[2048,1024]{1,0:T(8,128)(2,1)} %param.11), kind=kOutput, calls=%fused_computation.1 | convolution fusion | flops 134250496 | bytes 4390912 | tf_op jit(solution)/shard_map/dot_general | solution.py:220
  107.0 6.6 %all-to-all-done.4 = bf16[8,112,128]{2,1,0:T(8,128)(2,1)S(1)} async-done(((bf16[8,112,128]{2,1,0:T(8,128)(2,1)}), bf16[8,112,128]{2,1,0:T(8,128)(2,1)S(1)}, u32[]{:S(2)}, u32[]{:S(2)}) %all-to-all-start.4) | async-done | bytes 229408 | tf_op jit(solution)/shard_map/all_to_all | solution.py:159
  113.7 0.8 reshape.77
  (56 shorter events, 5.2 us)
Async XLA Ops:
  0.6 10.1 %collective-permute-start = (bf16[24,32768]{1,0:T(8,128)(2,1)}, bf16[24,32768]{1,0:T(8,128)(2,1)}, u32[]{:S(2)}, u32[]{:S(2)}) collective-permute-start(bf16[24,32768]{1,0:T(8,128)(2,1)} %own_ref.1), channel_id=1, source_target_pairs={{0,8},{8,0},{1,9},{9,1},{2,10},{10,2},{3,11},{11,3},{4,12},{12,4},... | collective-permute-start | bytes 4718600 | tf_op jit(solution)/shard_map/ppermute | solution.py:155
  1.6 8.9 %copy-start.3 = (s32[1,2048]{1,0:T(1,128)S(1)}, s32[1,2048]{1,0:T(1,128)}, u32[]{:S(2)}) copy-start(s32[1,2048]{1,0:T(1,128)} %param.14) | copy-start | bytes 24580
  1.7 8.9 %copy-start.7 = (s32[1,2048,16]{1,2,0:T(8,128)S(1)}, s32[1,2048,16]{1,2,0:T(8,128)}, u32[]{:S(2)}) copy-start(s32[1,2048,16]{1,2,0:T(8,128)} %param.13) | copy-start | bytes 393220
  3.0 7.7 %copy-start = (bf16[24,32768]{1,0:T(8,128)(2,1)S(1)}, bf16[24,32768]{1,0:T(8,128)(2,1)}, u32[]{:S(2)}) copy-start(bf16[24,32768]{1,0:T(8,128)(2,1)} %own_ref.1) | copy-start | bytes 4718596
  3.0 7.7 %copy-start.4 = (s32[1,2048]{1,0:T(1,128)S(1)}, s32[1,2048]{1,0:T(1,128)}, u32[]{:S(2)}) copy-start(s32[1,2048]{1,0:T(1,128)} %param.12) | copy-start | bytes 24580
  3.0 31.4 %all-to-all-start = ((bf16[16,48,1024]{2,1,0:T(8,128)(2,1)}), bf16[16,48,1024]{2,1,0:T(8,128)(2,1)S(1)}, u32[]{:S(2)}, u32[]{:S(2)}) async-start(bf16[16,48,1024]{2,1,0:T(8,128)(2,1)} %broadcast_in_dim.28), calls=%async_computation | async-start | bytes 3145728 | tf_op jit(solution)/shard_map/all_to_all | solution.py:159
  10.7 30.1 %copy-start.6 = (bf16[1,32,1024]{2,1,0:T(8,128)(2,1)S(1)}, bf16[1,32,1024]{2,1,0:T(8,128)(2,1)}, u32[]{:S(2)}) copy-start(bf16[1,32,1024]{2,1,0:T(8,128)(2,1)} %param.17) | copy-start | bytes 196612
  34.4 13.6 %collective-permute-start.1 = (bf16[16,48,1024]{2,1,0:T(8,128)(2,1)S(1)}, bf16[16,48,1024]{2,1,0:T(8,128)(2,1)S(1)}, u32[]{:S(2)}, u32[]{:S(2)}) collective-permute-start(bf16[16,48,1024]{2,1,0:T(8,128)(2,1)S(1)} %all-to-all-done.mine_ref), channel_id=1, source_target_pairs={{0,8},{8,0},{1,9},{9,1},{2,10},{10,2},{3,11},{11,3},{4,12},{12,4},... | collective-permute-start | bytes 4718600 | tf_op jit(solution)/shard_map/ppermute | solution.py:155
  34.4 13.6 %all-to-all-start.1 = ((bf16[16,64,96]{2,1,0:T(8,128)(2,1)}), bf16[16,64,96]{2,1,0:T(8,128)(2,1)}, u32[]{:S(2)}, u32[]{:S(2)}) async-start(bf16[16,64,96]{2,1,0:T(8,128)(2,1)} %get-tuple-element.20), calls=%async_computation.1 | async-start | bytes 524288 | tf_op jit(solution)/shard_map/all_to_all | solution.py:159
  40.8 3.6 %copy-start.5 = (s32[1,32]{1,0:T(1,128)S(1)}, s32[1,32]{1,0:T(1,128)}, u32[]{:S(2)}) copy-start(s32[1,32]{1,0:T(1,128)} %count_ref.1) | copy-start | bytes 388
  40.8 3.6 %copy-start.8 = (s32[1,32,8]{1,2,0:T(8,128)S(1)}, s32[1,32,8]{1,2,0:T(8,128)}, u32[]{:S(2)}) copy-start(s32[1,32,8]{1,2,0:T(8,128)} %param.15) | copy-start | bytes 3076
  50.0 0.8 copy-start.1
  50.9 0.7 copy-start.2
  51.5 16.3 %all-to-all-start.2 = ((bf16[4,64,1024]{2,1,0:T(8,128)(2,1)}), bf16[4,64,1024]{2,1,0:T(8,128)(2,1)S(1)}, u32[]{:S(2)}, u32[]{:S(2)}) async-start(bf16[4,64,1024]{2,1,0:T(8,128)(2,1)} %copy-done.1), calls=%async_computation.2 | async-start | bytes 1048576 | tf_op jit(solution)/shard_map/all_to_all | solution.py:159
  56.9 7.1 %collective-permute-start.2 = (bf16[80,1024]{1,0:T(8,128)(2,1)S(1)}, bf16[80,1024]{1,0:T(8,128)(2,1)S(1)}, u32[]{:S(2)}, u32[]{:S(2)}) collective-permute-start(bf16[80,1024]{1,0:T(8,128)(2,1)S(1)} %get-tuple-element.54), channel_id=1, source_target_pairs={{0,16},{16,32},{32,48},{48,0},{1,17},{17,33},{33,49},{49,1},{2,18}... | collective-permute-start | bytes 491528 | tf_op jit(solution)/shard_map/ppermute | solution.py:165
  57.9 8.2 %collective-permute-start.3 = (bf16[80,1024]{1,0:T(8,128)(2,1)S(1)}, bf16[80,1024]{1,0:T(8,128)(2,1)S(1)}, u32[]{:S(2)}, u32[]{:S(2)}) collective-permute-start(bf16[80,1024]{1,0:T(8,128)(2,1)S(1)} %get-tuple-element.55), channel_id=1, source_target_pairs={{0,32},{16,48},{32,0},{48,16},{1,33},{17,49},{33,1},{49,17},{2,34}... | collective-permute-start | bytes 491528 | tf_op jit(solution)/shard_map/ppermute | solution.py:165
  60.6 7.2 %collective-permute-start.4 = (bf16[80,1024]{1,0:T(8,128)(2,1)S(1)}, bf16[80,1024]{1,0:T(8,128)(2,1)S(1)}, u32[]{:S(2)}, u32[]{:S(2)}) collective-permute-start(bf16[80,1024]{1,0:T(8,128)(2,1)S(1)} %get-tuple-element.53), channel_id=1, source_target_pairs={{0,48},{16,0},{32,16},{48,32},{1,49},{17,1},{33,17},{49,33},{2,50}... | collective-permute-start | bytes 491528 | tf_op jit(solution)/shard_map/ppermute | solution.py:165
  68.5 1.8 %collective-permute-start.5 = (bf16[4,48,1024]{2,1,0:T(8,128)(2,1)S(1)}, bf16[4,48,1024]{2,1,0:T(8,128)(2,1)S(1)}, u32[]{:S(2)}, u32[]{:S(2)}) collective-permute-start(bf16[4,48,1024]{2,1,0:T(8,128)(2,1)S(1)} %fusion.6), channel_id=1, source_target_pairs={{0,8},{8,0},{1,9},{9,1},{2,10},{10,2},{3,11},{11,3},{4,12},{12,4},... | collective-permute-start | bytes 1179656 | tf_op jit(solution)/shard_map/ppermute | solution.py:155
  71.9 12.1 %collective-permute-start.6 = (bf16[4,64,1024]{2,1,0:T(8,128)(2,1)S(1)}, bf16[4,64,1024]{2,1,0:T(8,128)(2,1)}, u32[]{:S(2)}, u32[]{:S(2)}) collective-permute-start(bf16[4,64,1024]{2,1,0:T(8,128)(2,1)S(1)} %fusion.3), channel_id=1, source_target_pairs={{0,8},{8,0},{1,9},{9,1},{2,10},{10,2},{3,11},{11,3},{4,12},{12,4},... | collective-permute-start | bytes 1572872 | tf_op jit(solution)/shard_map/ppermute | solution.py:155
  72.2 25.4 %all-to-all-start.3 = ((bf16[32,48,128]{2,1,0:T(8,128)(2,1)}), bf16[32,48,128]{2,1,0:T(8,128)(2,1)S(1)}, u32[]{:S(2)}, u32[]{:S(2)}) async-start(bf16[32,48,128]{2,1,0:T(8,128)(2,1)} %bitcast.33), calls=%async_computation.3 | async-start | bytes 786432 | tf_op jit(solution)/shard_map/all_to_all | solution.py:159
  85.3 6.5 %collective-permute-start.7 = (bf16[64,1024]{1,0:T(8,128)(2,1)S(1)}, bf16[64,1024]{1,0:T(8,128)(2,1)S(1)}, u32[]{:S(2)}, u32[]{:S(2)}) collective-permute-start(bf16[64,1024]{1,0:T(8,128)(2,1)S(1)} %get-tuple-element.38), channel_id=1, source_target_pairs={{0,64},{64,128},{128,192},{192,0},{1,65},{65,129},{129,193},{193,1... | collective-permute-start | bytes 393224 | tf_op jit(solution)/shard_map/ppermute | solution.py:165
  87.1 8.7 %collective-permute-start.8 = (bf16[64,1024]{1,0:T(8,128)(2,1)S(1)}, bf16[64,1024]{1,0:T(8,128)(2,1)S(1)}, u32[]{:S(2)}, u32[]{:S(2)}) collective-permute-start(bf16[64,1024]{1,0:T(8,128)(2,1)S(1)} %get-tuple-element.40), channel_id=1, source_target_pairs={{0,128},{64,192},{128,0},{192,64},{1,129},{65,193},{129,1},{193,65... | collective-permute-start | bytes 393224 | tf_op jit(solution)/shard_map/ppermute | solution.py:165
  89.8 6.0 %collective-permute-start.9 = (bf16[64,1024]{1,0:T(8,128)(2,1)S(1)}, bf16[64,1024]{1,0:T(8,128)(2,1)S(1)}, u32[]{:S(2)}, u32[]{:S(2)}) collective-permute-start(bf16[64,1024]{1,0:T(8,128)(2,1)S(1)} %get-tuple-element.39), channel_id=1, source_target_pairs={{0,192},{64,0},{128,64},{192,128},{1,193},{65,1},{129,65},{193,129... | collective-permute-start | bytes 393224 | tf_op jit(solution)/shard_map/ppermute | solution.py:165
  98.3 15.3 %all-to-all-start.4 = ((bf16[8,112,128]{2,1,0:T(8,128)(2,1)}), bf16[8,112,128]{2,1,0:T(8,128)(2,1)S(1)}, u32[]{:S(2)}, u32[]{:S(2)}) async-start(bf16[8,112,128]{2,1,0:T(8,128)(2,1)} %pad_maximum_fusion.8), calls=%async_computation.4 | async-start | bytes 458752 | tf_op jit(solution)/shard_map/all_to_all | solution.py:159

commit v4 on v3

--- a/solution.py
+++ b/solution.py
@@ -214,24 +214,29 @@
     grad_joined = lax.dot_general(late_upstream, second_weight, (((1,), (1,)), ((), ())), preferred_element_type=F32)
     inner = jnp.where(jnp.arange(fan_inner, dtype=jnp.int32)[:, None] < inner_count, inner, owner_rows)
     owned = exchange(stacked, ("x", "y"))
+    far = ny // 2
+    upstream_far = lax.ppermute(upstream, "y", [(i, (i + far) % ny) for i in range(ny)])
+    owned, upstream_far = lax.optimization_barrier((owned, upstream_far))
     message, joined, pieces = owner_kernel(nx, ny, owner_rows, second_rows, fan_inner, width, both)(
         place, owned, weight_mine, weight_other, inner, inner_counts, grad_joined
     )
     output = jnp.dot(joined, second_weight, preferred_element_type=F32).astype(BF16)
     folded = second_rows // 2
-    packed = [jnp.concatenate([pieces[k], upstream, relative[k]], axis=0) for k in range(ny)]
+    packed = [
+        jnp.concatenate([pieces[k], relative[k]] + [upstream] * (k != far), axis=0) for k in range(ny)
+    ]
     grad_pre_x = exchange(message, "x").reshape(nx * owner_rows, width)
     packed, in_order = turn_blocks(packed, "y")
     grad_pre_x, packed = lax.optimization_barrier((grad_pre_x, packed))
-    along_y = in_order([block[folded + second_rows :] for block in packed])
+    turned = folded + relative.shape[1]
+    along_y = in_order([block[folded:turned] for block in packed])
     along_y = along_y.reshape(ny, -1, width // LANES, LANES).transpose(0, 2, 1, 3)
     along_y = along_y.reshape(ny, nx * owner_rows, LANES)[:, :, : 2 * both]
-    packed = jnp.stack(packed)
-    columns_y = packed[:, :folded]
+    columns_y = jnp.stack([block[:folded] for block in packed])
     chunk = columns_y.shape[2] // 2
     columns_y = jnp.concatenate([columns_y[:, :, :chunk], columns_y[:, :, chunk:]], axis=1)
     columns_y = columns_y.reshape(ny * second_rows, chunk)
-    upstream_y = packed[:, folded : folded + second_rows].reshape(ny * second_rows, width)
+    upstream_y = jnp.concatenate([upstream_far if k == far else packed[k][turned:] for k in range(ny)], axis=0)
     first_terms = lax.dot_general(
         along_y, grad_pre_x, (((1,), (0,)), ((), ())), preferred_element_type=F32
     ).reshape(ny, 2, both, width)

time: 117 us -> 117 us (level)
  waiting for transfers between devices: 26.6 us -> 24.1 us
  starting transfers between devices: 43.9 us -> 45.7 us
    all_to_all x5, waiting for transfers between devices: 13.4 us -> 11.3 us  [exchange(): return lax.all_to_all(values, axis, split_axis=0, concat_axis=0, tiled=True)]
    all_to_all x5, starting transfers between devices: 33.6 us -> 35.2 us  [exchange(): return lax.all_to_all(values, axis, split_axis=0, concat_axis=0, tiled=True)]
  transfers between devices with their start and end apart: 15 -> 16, of which waited for: 10 -> 8; matrix products, arithmetic and copies ran while one was open for 12% -> 12% of each run, Pallas kernels for 19% -> 19%
where the time goes in v4:
time: 117 us; the launch traced here: 116 us
  starting transfers between devices  45.7 us (39%)
  Pallas kernels  24.2 us (21%)
  waiting for transfers between devices  24.1 us (21%)
  matrix products  8.87 us (8%)
  local copies, waits for them, and re-layouts  7.32 us (6%)
  other arithmetic  4.83 us (4%)
    all_to_all x5, starting transfers between devices, exchange(): return lax.all_to_all(values, axis, split_axis=0, concat_axis=0, tiled=True)  35.2 us
    pallas_call x1, Pallas kernels, body(): gather_kernel(slots, nx * ny, ny, owner_rows, slice_width, nodes, width)  22.2 us
    all_to_all x5, waiting for transfers between devices, exchange(): return lax.all_to_all(values, axis, split_axis=0, concat_axis=0, tiled=True)  11.3 us
    ppermute x6, waiting for transfers between devices, turn_blocks(): lax.ppermute(blocks[k], axis, [(i, (i + k) % n) for i in range(n)])  11.2 us
    ppermute x6, starting transfers between devices, turn_blocks(): lax.ppermute(blocks[k], axis, [(i, (i + k) % n) for i in range(n)])  9.1 us
    dot_general x1, matrix products, body(): jnp.dot(joined, second_weight, preferred_element_type=F32).astype(BF16)  3.65 us
    dot_general x1, matrix products, body(): lax.dot_general(late_upstream, second_weight, (((1,), (1,)), ((), ())), p...  3.54 us
    unnamed x23, local copies, waits for them, and re-layouts  3.33 us
  transfers between devices with their start and end apart: 16, of which 8 were waited for; matrix products, arithmetic and copies ran while one was open for 12% of the time, Pallas kernels for 19%

profile of v4, /device:TPU:8, one launch (start us, length us, event | category | flops | bytes accessed | tf_op | source)
XLA Modules:
  0.0 116.0 jit_solution(9142065757704820043)
XLA Ops:
  0.7 0.9 copy.16
  1.7 1.3 %broadcast_in_dim.28 = bf16[16,48,1024]{2,1,0:T(8,128)(2,1)} broadcast(bf16[48,1024]{1,0:T(8,128)(2,1)S(1)} %bitcast.140), dimensions={1,2} | broadcast | bytes 1671168 | tf_op jit(solution)/shard_map/broadcast_in_dim | solution.py:195
  3.0 7.5 %all-to-all-start = ((bf16[16,48,1024]{2,1,0:T(8,128)(2,1)}), bf16[16,48,1024]{2,1,0:T(8,128)(2,1)S(1)}, u32[]{:S(2)}, u32[]{:S(2)}) async-start(bf16[16,48,1024]{2,1,0:T(8,128)(2,1)} %broadcast_in_dim.28), calls=%async_computation | async-start | bytes 3145728 | tf_op jit(solution)/shard_map/all_to_all | solution.py:159
  10.7 22.2 %gather_mean.1 = (bf16[16,64,96]{2,1,0:T(8,128)(2,1)}, bf16[4,32,1024]{2,1,0:T(8,128)(2,1)S(1)}) custom-call(s32[2]{0:T(128)S(1)} %pad_add_fusion.place_ref, s32[32768]{0:T(1024)S(1)} %bitcast.126, s32[2048]{0:T(1024)S(1)} %bitcast.129, s32[2048]{0:T(1024)S(1)} %bitcast.128, bf16[24,32768]{1,0:T(8,128)(2,1)S(1)} %copy-done, ...), custom_call_target="tpu_custom_call" | custom-call | flops 50000000 | bytes 100000000 | tf_op jit(solution)/shard_map/gather_mean/pallas_call | solution.py:201
  32.9 1.5 %all-to-all-done.mine_ref = bf16[16,48,1024]{2,1,0:T(8,128)(2,1)S(1)} async-done(((bf16[16,48,1024]{2,1,0:T(8,128)(2,1)}), bf16[16,48,1024]{2,1,0:T(8,128)(2,1)S(1)}, u32[]{:S(2)}, u32[]{:S(2)}) %all-to-all-start) | async-done | bytes 1572896 | tf_op jit(solution)/shard_map/all_to_all | solution.py:159
  34.4 1.0 collective-permute-start.1
  35.4 6.0 %all-to-all-start.1 = ((bf16[16,64,96]{2,1,0:T(8,128)(2,1)}), bf16[16,64,96]{2,1,0:T(8,128)(2,1)}, u32[]{:S(2)}, u32[]{:S(2)}) async-start(bf16[16,64,96]{2,1,0:T(8,128)(2,1)} %get-tuple-element.22), calls=%async_computation.1 | async-start | bytes 524288 | tf_op jit(solution)/shard_map/all_to_all | solution.py:159
  42.1 3.5 %fusion.27.grad_ref = f32[32,2048]{1,0:T(8,128)S(1)} fusion(bf16[32,1024]{1,0:T(8,128)(2,1)S(1)} %bitcast.144, bf16[2048,1024]{1,0:T(8,128)(2,1)} %param.11), kind=kOutput, calls=%fused_computation.73 | convolution fusion | flops 134217728 | bytes 4521984 | tf_op jit(solution)/shard_map/dot_general | solution.py:214
  45.7 3.1 %all-to-all-done.1.owned_ref = bf16[16,64,96]{2,1,0:T(8,128)(2,1)} async-done(((bf16[16,64,96]{2,1,0:T(8,128)(2,1)}), bf16[16,64,96]{2,1,0:T(8,128)(2,1)}, u32[]{:S(2)}, u32[]{:S(2)}) %all-to-all-start.1) | async-done | bytes 196640 | tf_op jit(solution)/shard_map/all_to_all | solution.py:159
  48.8 2.0 %owner_layers.1 = (bf16[4,64,1024]{2,1,0:T(8,128)(2,1)S(1)}, bf16[32,2048]{1,0:T(8,128)(2,1)S(1)}, bf16[4,16,1024]{2,1,0:T(8,128)(2,1)S(1)}) custom-call(s32[2]{0:T(128)S(1)} %pad_add_fusion.place_ref, bf16[16,64,96]{2,1,0:T(8,128)(2,1)} %all-to-all-done.1.owned_ref, bf16[16,48,1024]{2,1,0:T(8,128)(2,1)S(1)} %all-to-all-done.mine_ref, ...), custom_call_target="tpu_custom_call" | custom-call | flops 350000000 | bytes 9000000 | tf_op jit(solution)/shard_map/owner_layers/pallas_call | solution.py:220
  50.9 0.8 copy-done.1
  52.3 3.5 %all-to-all-start.2 = ((bf16[4,64,1024]{2,1,0:T(8,128)(2,1)}), bf16[4,64,1024]{2,1,0:T(8,128)(2,1)S(1)}, u32[]{:S(2)}, u32[]{:S(2)}) async-start(bf16[4,64,1024]{2,1,0:T(8,128)(2,1)} %copy-done.1), calls=%async_computation.2 | async-start | bytes 1048576 | tf_op jit(solution)/shard_map/all_to_all | solution.py:159
  55.8 0.8 slice_bitcast_fusion.12
  56.6 1.0 pad_maximum_fusion.2
  57.6 1.1 collective-permute-start.3
  58.7 1.0 collective-permute-start.5
  59.7 0.8 pad_maximum_fusion.7
  60.6 1.6 %collective-permute-start.4 = (bf16[48,1024]{1,0:T(8,128)(2,1)S(1)}, bf16[48,1024]{1,0:T(8,128)(2,1)S(1)}, u32[]{:S(2)}, u32[]{:S(2)}) collective-permute-start(bf16[48,1024]{1,0:T(8,128)(2,1)S(1)} %pad_maximum_fusion.7), channel_id=1, source_target_pairs={{0,32},{16,48},{32,0},{48,16},{1,33},{17,49},{33,1},{49,17},{2,34}... | collective-permute-start | bytes 294920 | tf_op jit(solution)/shard_map/ppermute | solution.py:165
  62.2 4.6 %collective-permute-done.4 = bf16[48,1024]{1,0:T(8,128)(2,1)S(1)} collective-permute-done((bf16[48,1024]{1,0:T(8,128)(2,1)S(1)}, bf16[48,1024]{1,0:T(8,128)(2,1)S(1)}, u32[]{:S(2)}, u32[]{:S(2)}) %collective-permute-start.4) | collective-permute-done | bytes 98336 | tf_op jit(solution)/shard_map/ppermute | solution.py:165
  67.6 1.6 %collective-permute-done.6 = bf16[4,48,1024]{2,1,0:T(8,128)(2,1)S(1)} collective-permute-done((bf16[4,48,1024]{2,1,0:T(8,128)(2,1)S(1)}, bf16[4,48,1024]{2,1,0:T(8,128)(2,1)S(1)}, u32[]{:S(2)}, u32[]{:S(2)}) %collective-permute-start.6) | collective-permute-done | bytes 393248 | tf_op jit(solution)/shard_map/ppermute | solution.py:155
  69.5 0.8 copy.20
  70.3 1.3 %fusion.8 = f32[512,1024]{1,0:T(8,128)S(1)} fusion(bf16[128,512]{1,0:T(8,128)(2,1)S(1)} %bitcast.139, bf16[32,1024]{1,0:T(8,128)(2,1)S(1)} %get-tuple-element.57, bf16[32,1024]{1,0:T(8,128)(2,1)} %collective-permute-done.1, bf16[32,1024]{1,0:T(8,128)(2,1)S(1)} %get-tuple-element.73, bf16[32,1024]{1,0:T(8,128)(2,1)S(1)} %get-tuple-element.53), kind=kOutput, calls=%fused_computation.17 | convolution fusion | flops 135266304 | bytes 2490368 | tf_op jit(solution)/shard_map/dot_general | solution.py:253
  71.9 11.6 %all-to-all-start.3 = ((bf16[32,48,128]{2,1,0:T(8,128)(2,1)}), bf16[32,48,128]{2,1,0:T(8,128)(2,1)S(1)}, u32[]{:S(2)}, u32[]{:S(2)}) async-start(bf16[32,48,128]{2,1,0:T(8,128)(2,1)} %bitcast.33), calls=%async_computation.3 | async-start | bytes 786432 | tf_op jit(solution)/shard_map/all_to_all | solution.py:159
  83.6 1.2 %fusion.1 = bf16[4,64,1024]{2,1,0:T(8,128)(2,1)S(1)} fusion(bf16[4,64,1024]{2,1,0:T(8,128)(2,1)} %collective-permute-done.7, f32[4,2,64,1024]{3,2,1,0:T(8,128)S(1)} %bitcast.132, s32[]{:T(128)S(6)} %select_n.89), kind=kLoop, calls=%fused_computation.3 | loop fusion | flops 786432 | bytes 2097156 | tf_op jit(solution)/shard_map/convert_element_type | solution.py:258
  84.8 3.0 %collective-permute-start.10 = (bf16[64,1024]{1,0:T(8,128)(2,1)S(1)}, bf16[64,1024]{1,0:T(8,128)(2,1)S(1)}, u32[]{:S(2)}, u32[]{:S(2)}) collective-permute-start(bf16[64,1024]{1,0:T(8,128)(2,1)S(1)} %get-tuple-element.43), channel_id=1, source_target_pairs={{0,192},{64,0},{128,64},{192,128},{1,193},{65,1},{129,65},{193,129... | collective-permute-start | bytes 393224 | tf_op jit(solution)/shard_map/ppermute | solution.py:165
  87.9 2.3 %collective-permute-start.9 = (bf16[64,1024]{1,0:T(8,128)(2,1)S(1)}, bf16[64,1024]{1,0:T(8,128)(2,1)S(1)}, u32[]{:S(2)}, u32[]{:S(2)}) collective-permute-start(bf16[64,1024]{1,0:T(8,128)(2,1)S(1)} %get-tuple-element.44), channel_id=1, source_target_pairs={{0,128},{64,192},{128,0},{192,64},{1,129},{65,193},{129,1},{193,65... | collective-permute-start | bytes 393224 | tf_op jit(solution)/shard_map/ppermute | solution.py:165
  90.6 6.2 %collective-permute-done.8 = bf16[64,1024]{1,0:T(8,128)(2,1)S(1)} collective-permute-done((bf16[64,1024]{1,0:T(8,128)(2,1)S(1)}, bf16[64,1024]{1,0:T(8,128)(2,1)S(1)}, u32[]{:S(2)}, u32[]{:S(2)}) %collective-permute-start.8) | collective-permute-done | bytes 131104 | tf_op jit(solution)/shard_map/ppermute | solution.py:165
  97.1 0.7 pad_maximum_fusion.1
  97.8 6.5 %all-to-all-start.4 = ((bf16[8,112,128]{2,1,0:T(8,128)(2,1)}), bf16[8,112,128]{2,1,0:T(8,128)(2,1)S(1)}, u32[]{:S(2)}, u32[]{:S(2)}) async-start(bf16[8,112,128]{2,1,0:T(8,128)(2,1)} %pad_maximum_fusion.1), calls=%async_computation.4 | async-start | bytes 458752 | tf_op jit(solution)/shard_map/all_to_all | solution.py:159
  104.4 3.6 %fusion = bf16[1,32,1024]{2,1,0:T(8,128)(2,1)} fusion(bf16[32,2048]{1,0:T(8,128)(2,1)S(1)} %get-tuple-element.29, bf16[2048,1024]{1,0:T(8,128)(2,1)} %param.11), kind=kOutput, calls=%fused_computation.1 | convolution fusion | flops 134250496 | bytes 4390912 | tf_op jit(solution)/shard_map/dot_general | solution.py:223
  108.0 6.5 %all-to-all-done.4 = bf16[8,112,128]{2,1,0:T(8,128)(2,1)S(1)} async-done(((bf16[8,112,128]{2,1,0:T(8,128)(2,1)}), bf16[8,112,128]{2,1,0:T(8,128)(2,1)S(1)}, u32[]{:S(2)}, u32[]{:S(2)}) %all-to-all-start.4) | async-done | bytes 229408 | tf_op jit(solution)/shard_map/all_to_all | solution.py:159
  114.6 0.8 reshape.74
  (62 shorter events, 4.4 us)
Async XLA Ops:
  0.6 10.1 %collective-permute-start = (bf16[24,32768]{1,0:T(8,128)(2,1)}, bf16[24,32768]{1,0:T(8,128)(2,1)}, u32[]{:S(2)}, u32[]{:S(2)}) collective-permute-start(bf16[24,32768]{1,0:T(8,128)(2,1)} %own_ref.1), channel_id=1, source_target_pairs={{0,8},{8,0},{1,9},{9,1},{2,10},{10,2},{3,11},{11,3},{4,12},{12,4},... | collective-permute-start | bytes 4718600 | tf_op jit(solution)/shard_map/ppermute | solution.py:155
  1.6 8.9 %copy-start.3 = (s32[1,2048]{1,0:T(1,128)S(1)}, s32[1,2048]{1,0:T(1,128)}, u32[]{:S(2)}) copy-start(s32[1,2048]{1,0:T(1,128)} %param.14) | copy-start | bytes 24580
  1.7 8.9 %copy-start.7 = (s32[1,2048,16]{1,2,0:T(8,128)S(1)}, s32[1,2048,16]{1,2,0:T(8,128)}, u32[]{:S(2)}) copy-start(s32[1,2048,16]{1,2,0:T(8,128)} %param.13) | copy-start | bytes 393220
  3.0 7.7 %copy-start = (bf16[24,32768]{1,0:T(8,128)(2,1)S(1)}, bf16[24,32768]{1,0:T(8,128)(2,1)}, u32[]{:S(2)}) copy-start(bf16[24,32768]{1,0:T(8,128)(2,1)} %own_ref.1) | copy-start | bytes 4718596
  3.0 7.7 %copy-start.4 = (s32[1,2048]{1,0:T(1,128)S(1)}, s32[1,2048]{1,0:T(1,128)}, u32[]{:S(2)}) copy-start(s32[1,2048]{1,0:T(1,128)} %param.12) | copy-start | bytes 24580
  3.0 31.4 %all-to-all-start = ((bf16[16,48,1024]{2,1,0:T(8,128)(2,1)}), bf16[16,48,1024]{2,1,0:T(8,128)(2,1)S(1)}, u32[]{:S(2)}, u32[]{:S(2)}) async-start(bf16[16,48,1024]{2,1,0:T(8,128)(2,1)} %broadcast_in_dim.28), calls=%async_computation | async-start | bytes 3145728 | tf_op jit(solution)/shard_map/all_to_all | solution.py:159
  10.5 23.8 %copy-start.6 = (bf16[1,32,1024]{2,1,0:T(8,128)(2,1)S(1)}, bf16[1,32,1024]{2,1,0:T(8,128)(2,1)}, u32[]{:S(2)}) copy-start(bf16[1,32,1024]{2,1,0:T(8,128)(2,1)} %param.17) | copy-start | bytes 196612
  34.4 14.4 %collective-permute-start.2 = (bf16[16,48,1024]{2,1,0:T(8,128)(2,1)S(1)}, bf16[16,48,1024]{2,1,0:T(8,128)(2,1)S(1)}, u32[]{:S(2)}, u32[]{:S(2)}) collective-permute-start(bf16[16,48,1024]{2,1,0:T(8,128)(2,1)S(1)} %all-to-all-done.mine_ref), channel_id=1, source_target_pairs={{0,8},{8,0},{1,9},{9,1},{2,10},{10,2},{3,11},{11,3},{4,12},{12,4},... | collective-permute-start | bytes 4718600 | tf_op jit(solution)/shard_map/ppermute | solution.py:155
  34.4 11.3 %collective-permute-start.1 = (bf16[32,1024]{1,0:T(8,128)(2,1)S(1)}, bf16[32,1024]{1,0:T(8,128)(2,1)}, u32[]{:S(2)}, u32[]{:S(2)}) collective-permute-start(bf16[32,1024]{1,0:T(8,128)(2,1)S(1)} %bitcast.143), channel_id=1, source_target_pairs={{0,32},{16,48},{32,0},{48,16},{1,33},{17,49},{33,1},{49,17},{2,34}... | collective-permute-start | bytes 196616 | tf_op jit(solution)/shard_map/ppermute | solution.py:218
  35.4 13.5 %all-to-all-start.1 = ((bf16[16,64,96]{2,1,0:T(8,128)(2,1)}), bf16[16,64,96]{2,1,0:T(8,128)(2,1)}, u32[]{:S(2)}, u32[]{:S(2)}) async-start(bf16[16,64,96]{2,1,0:T(8,128)(2,1)} %get-tuple-element.22), calls=%async_computation.1 | async-start | bytes 524288 | tf_op jit(solution)/shard_map/all_to_all | solution.py:159
  42.1 3.6 %copy-start.5 = (s32[1,32]{1,0:T(1,128)S(1)}, s32[1,32]{1,0:T(1,128)}, u32[]{:S(2)}) copy-start(s32[1,32]{1,0:T(1,128)} %count_ref.1) | copy-start | bytes 388
  42.1 3.6 %copy-start.8 = (s32[1,32,8]{1,2,0:T(8,128)S(1)}, s32[1,32,8]{1,2,0:T(8,128)}, u32[]{:S(2)}) copy-start(s32[1,32,8]{1,2,0:T(8,128)} %param.15) | copy-start | bytes 3076
  50.9 0.8 copy-start.1
  51.7 0.7 copy-start.2
  52.3 14.4 %all-to-all-start.2 = ((bf16[4,64,1024]{2,1,0:T(8,128)(2,1)}), bf16[4,64,1024]{2,1,0:T(8,128)(2,1)S(1)}, u32[]{:S(2)}, u32[]{:S(2)}) async-start(bf16[4,64,1024]{2,1,0:T(8,128)(2,1)} %copy-done.1), calls=%async_computation.2 | async-start | bytes 1048576 | tf_op jit(solution)/shard_map/all_to_all | solution.py:159
  57.6 9.1 %collective-permute-start.3 = (bf16[80,1024]{1,0:T(8,128)(2,1)S(1)}, bf16[80,1024]{1,0:T(8,128)(2,1)S(1)}, u32[]{:S(2)}, u32[]{:S(2)}) collective-permute-start(bf16[80,1024]{1,0:T(8,128)(2,1)S(1)} %get-tuple-element.66), channel_id=1, source_target_pairs={{0,16},{16,32},{32,48},{48,0},{1,17},{17,33},{33,49},{49,1},{2,18}... | collective-permute-start | bytes 491528 | tf_op jit(solution)/shard_map/ppermute | solution.py:165
  58.7 8.1 %collective-permute-start.5 = (bf16[80,1024]{1,0:T(8,128)(2,1)S(1)}, bf16[80,1024]{1,0:T(8,128)(2,1)S(1)}, u32[]{:S(2)}, u32[]{:S(2)}) collective-permute-start(bf16[80,1024]{1,0:T(8,128)(2,1)S(1)} %get-tuple-element.65), channel_id=1, source_target_pairs={{0,48},{16,0},{32,16},{48,32},{1,49},{17,1},{33,17},{49,33},{2,50}... | collective-permute-start | bytes 491528 | tf_op jit(solution)/shard_map/ppermute | solution.py:165
  60.6 6.2 %collective-permute-start.4 = (bf16[48,1024]{1,0:T(8,128)(2,1)S(1)}, bf16[48,1024]{1,0:T(8,128)(2,1)S(1)}, u32[]{:S(2)}, u32[]{:S(2)}) collective-permute-start(bf16[48,1024]{1,0:T(8,128)(2,1)S(1)} %pad_maximum_fusion.7), channel_id=1, source_target_pairs={{0,32},{16,48},{32,0},{48,16},{1,33},{17,49},{33,1},{49,17},{2,34}... | collective-permute-start | bytes 294920 | tf_op jit(solution)/shard_map/ppermute | solution.py:165
  67.5 1.8 %collective-permute-start.6 = (bf16[4,48,1024]{2,1,0:T(8,128)(2,1)S(1)}, bf16[4,48,1024]{2,1,0:T(8,128)(2,1)S(1)}, u32[]{:S(2)}, u32[]{:S(2)}) collective-permute-start(bf16[4,48,1024]{2,1,0:T(8,128)(2,1)S(1)} %fusion.6), channel_id=1, source_target_pairs={{0,8},{8,0},{1,9},{9,1},{2,10},{10,2},{3,11},{11,3},{4,12},{12,4},... | collective-permute-start | bytes 1179656 | tf_op jit(solution)/shard_map/ppermute | solution.py:155
  71.7 11.9 %collective-permute-start.7 = (bf16[4,64,1024]{2,1,0:T(8,128)(2,1)S(1)}, bf16[4,64,1024]{2,1,0:T(8,128)(2,1)}, u32[]{:S(2)}, u32[]{:S(2)}) collective-permute-start(bf16[4,64,1024]{2,1,0:T(8,128)(2,1)S(1)} %fusion.3), channel_id=1, source_target_pairs={{0,8},{8,0},{1,9},{9,1},{2,10},{10,2},{3,11},{11,3},{4,12},{12,4},... | collective-permute-start | bytes 1572872 | tf_op jit(solution)/shard_map/ppermute | solution.py:155
  71.9 25.1 %all-to-all-start.3 = ((bf16[32,48,128]{2,1,0:T(8,128)(2,1)}), bf16[32,48,128]{2,1,0:T(8,128)(2,1)S(1)}, u32[]{:S(2)}, u32[]{:S(2)}) async-start(bf16[32,48,128]{2,1,0:T(8,128)(2,1)} %bitcast.33), calls=%async_computation.3 | async-start | bytes 786432 | tf_op jit(solution)/shard_map/all_to_all | solution.py:159
  84.8 5.8 %collective-permute-start.10 = (bf16[64,1024]{1,0:T(8,128)(2,1)S(1)}, bf16[64,1024]{1,0:T(8,128)(2,1)S(1)}, u32[]{:S(2)}, u32[]{:S(2)}) collective-permute-start(bf16[64,1024]{1,0:T(8,128)(2,1)S(1)} %get-tuple-element.43), channel_id=1, source_target_pairs={{0,192},{64,0},{128,64},{192,128},{1,193},{65,1},{129,65},{193,129... | collective-permute-start | bytes 393224 | tf_op jit(solution)/shard_map/ppermute | solution.py:165
  87.9 8.9 %collective-permute-start.8 = (bf16[64,1024]{1,0:T(8,128)(2,1)S(1)}, bf16[64,1024]{1,0:T(8,128)(2,1)S(1)}, u32[]{:S(2)}, u32[]{:S(2)}) collective-permute-start(bf16[64,1024]{1,0:T(8,128)(2,1)S(1)} %get-tuple-element.42), channel_id=1, source_target_pairs={{0,64},{64,128},{128,192},{192,0},{1,65},{65,129},{129,193},{193,1... | collective-permute-start | bytes 393224 | tf_op jit(solution)/shard_map/ppermute | solution.py:165
  87.9 8.9 %collective-permute-start.9 = (bf16[64,1024]{1,0:T(8,128)(2,1)S(1)}, bf16[64,1024]{1,0:T(8,128)(2,1)S(1)}, u32[]{:S(2)}, u32[]{:S(2)}) collective-permute-start(bf16[64,1024]{1,0:T(8,128)(2,1)S(1)} %get-tuple-element.44), channel_id=1, source_target_pairs={{0,128},{64,192},{128,0},{192,64},{1,129},{65,193},{129,1},{193,65... | collective-permute-start | bytes 393224 | tf_op jit(solution)/shard_map/ppermute | solution.py:165
  97.8 16.7 %all-to-all-start.4 = ((bf16[8,112,128]{2,1,0:T(8,128)(2,1)}), bf16[8,112,128]{2,1,0:T(8,128)(2,1)S(1)}, u32[]{:S(2)}, u32[]{:S(2)}) async-start(bf16[8,112,128]{2,1,0:T(8,128)(2,1)} %pad_maximum_fusion.1), calls=%async_computation.4 | async-start | bytes 458752 | tf_op jit(solution)/shard_map/all_to_all | solution.py:159

commit v5 on v4

--- a/solution.py
+++ b/solution.py
@@ -191,8 +191,7 @@
     both = 2 * slice_width
     upstream = cotangent[0]
 
-    weight = first_weight.transpose(1, 0, 2).reshape(both, width)
-    weight_mine = exchange(jnp.broadcast_to(weight[None], (nx * ny,) + weight.shape), ("x", "y"))
+    weight_mine = exchange(jnp.broadcast_to(first_weight[None], (nx * ny,) + first_weight.shape), ("x", "y"))
 
     counts = outer_counts[0]
     live = jnp.arange(slots, dtype=jnp.int32)[:, None] < counts[None, :]
@@ -207,6 +206,7 @@
         other_features,
     )
     stacked, weight_mine = lax.optimization_barrier((stacked, weight_mine))
+    weight_mine = weight_mine.transpose(0, 2, 1, 3).reshape(nx * ny, both, width)
     weight_other = swap(weight_mine)
     _, late_upstream, inner, inner_count = lax.optimization_barrier(
         (relative, upstream, inner_nodes[0].T, inner_counts)

time: 117 us -> 117 us (level)
  no operation moved by 1% of the time
where the time goes in v5:
time: 117 us; the launch traced here: 116 us
  starting transfers between devices  45.7 us (39%)
  Pallas kernels  24.2 us (21%)
  waiting for transfers between devices  24.1 us (21%)
  matrix products  8.87 us (8%)
  local copies, waits for them, and re-layouts  7.32 us (6%)
  other arithmetic  4.83 us (4%)
    all_to_all x5, starting transfers between devices, exchange(): return lax.all_to_all(values, axis, split_axis=0, concat_axis=0, tiled=True)  35.2 us
    pallas_call x1, Pallas kernels, body(): gather_kernel(slots, nx * ny, ny, owner_rows, slice_width, nodes, width)  22.2 us
    all_to_all x5, waiting for transfers between devices, exchange(): return lax.all_to_all(values, axis, split_axis=0, concat_axis=0, tiled=True)  11.3 us
    ppermute x6, waiting for transfers between devices, turn_blocks(): lax.ppermute(blocks[k], axis, [(i, (i + k) % n) for i in range(n)])  11.2 us
    ppermute x6, starting transfers between devices, turn_blocks(): lax.ppermute(blocks[k], axis, [(i, (i + k) % n) for i in range(n)])  9.1 us
    dot_general x1, matrix products, body(): jnp.dot(joined, second_weight, preferred_element_type=F32).astype(BF16)  3.65 us
    dot_general x1, matrix products, body(): lax.dot_general(late_upstream, second_weight, (((1,), (1,)), ((), ())), p...  3.54 us
    unnamed x23, local copies, waits for them, and re-layouts  3.33 us
  transfers between devices with their start and end apart: 16, of which 8 were waited for; matrix products, arithmetic and copies ran while one was open for 12% of the time, Pallas kernels for 19%

profile of v5, /device:TPU:8, one launch (start us, length us, event | category | flops | bytes accessed | tf_op | source)
XLA Modules:
  0.0 116.0 jit_solution(2055988307872146970)
XLA Ops:
  0.7 0.9 copy.17
  1.7 1.3 %broadcast_in_dim.26 = bf16[16,24,2,1024]{3,1,2,0:T(8,128)(2,1)} broadcast(bf16[24,2,1024]{2,0,1:T(8,128)(2,1)S(1)} %copy.17), dimensions={1,2,3} | broadcast | bytes 1671168 | tf_op jit(solution)/shard_map/broadcast_in_dim | solution.py:194
  3.0 7.5 %all-to-all-start = ((bf16[16,24,2,1024]{3,1,2,0:T(8,128)(2,1)}), bf16[16,24,2,1024]{3,1,2,0:T(8,128)(2,1)S(1)}, u32[]{:S(2)}, u32[]{:S(2)}) async-start(bf16[16,24,2,1024]{3,1,2,0:T(8,128)(2,1)} %broadcast_in_dim.26), calls=%async_computation | async-start | bytes 3145728 | tf_op jit(solution)/shard_map/all_to_all | solution.py:159
  10.7 22.2 %gather_mean.1 = (bf16[16,64,96]{2,1,0:T(8,128)(2,1)}, bf16[4,32,1024]{2,1,0:T(8,128)(2,1)S(1)}) custom-call(s32[2]{0:T(128)S(1)} %pad_add_fusion.place_ref, s32[32768]{0:T(1024)S(1)} %bitcast.128, s32[2048]{0:T(1024)S(1)} %bitcast.131, s32[2048]{0:T(1024)S(1)} %bitcast.130, bf16[24,32768]{1,0:T(8,128)(2,1)S(1)} %copy-done, ...), custom_call_target="tpu_custom_call" | custom-call | flops 50000000 | bytes 100000000 | tf_op jit(solution)/shard_map/gather_mean/pallas_call | solution.py:200
  32.9 1.5 %all-to-all-done = bf16[16,24,2,1024]{3,1,2,0:T(8,128)(2,1)S(1)} async-done(((bf16[16,24,2,1024]{3,1,2,0:T(8,128)(2,1)}), bf16[16,24,2,1024]{3,1,2,0:T(8,128)(2,1)S(1)}, u32[]{:S(2)}, u32[]{:S(2)}) %all-to-all-start) | async-done | bytes 1572896 | tf_op jit(solution)/shard_map/all_to_all | solution.py:159
  34.4 1.0 collective-permute-start.1
  35.4 6.0 %all-to-all-start.1 = ((bf16[16,64,96]{2,1,0:T(8,128)(2,1)}), bf16[16,64,96]{2,1,0:T(8,128)(2,1)}, u32[]{:S(2)}, u32[]{:S(2)}) async-start(bf16[16,64,96]{2,1,0:T(8,128)(2,1)} %get-tuple-element.22), calls=%async_computation.1 | async-start | bytes 524288 | tf_op jit(solution)/shard_map/all_to_all | solution.py:159
  42.1 3.5 %fusion.27.grad_ref = f32[32,2048]{1,0:T(8,128)S(1)} fusion(bf16[32,1024]{1,0:T(8,128)(2,1)S(1)} %bitcast.145, bf16[2048,1024]{1,0:T(8,128)(2,1)} %param.11), kind=kOutput, calls=%fused_computation.73 | convolution fusion | flops 134217728 | bytes 4521984 | tf_op jit(solution)/shard_map/dot_general | solution.py:214
  45.7 3.1 %all-to-all-done.1.owned_ref = bf16[16,64,96]{2,1,0:T(8,128)(2,1)} async-done(((bf16[16,64,96]{2,1,0:T(8,128)(2,1)}), bf16[16,64,96]{2,1,0:T(8,128)(2,1)}, u32[]{:S(2)}, u32[]{:S(2)}) %all-to-all-start.1) | async-done | bytes 196640 | tf_op jit(solution)/shard_map/all_to_all | solution.py:159
  48.8 2.0 %owner_layers.1 = (bf16[4,64,1024]{2,1,0:T(8,128)(2,1)S(1)}, bf16[32,2048]{1,0:T(8,128)(2,1)S(1)}, bf16[4,16,1024]{2,1,0:T(8,128)(2,1)S(1)}) custom-call(s32[2]{0:T(128)S(1)} %pad_add_fusion.place_ref, bf16[16,64,96]{2,1,0:T(8,128)(2,1)} %all-to-all-done.1.owned_ref, bf16[16,48,1024]{2,1,0:T(8,128)(2,1)S(1)} %bitcast.127, ...), custom_call_target="tpu_custom_call" | custom-call | flops 350000000 | bytes 9000000 | tf_op jit(solution)/shard_map/owner_layers/pallas_call | solution.py:220
  50.9 0.8 copy-done.1
  52.3 3.5 %all-to-all-start.2 = ((bf16[4,64,1024]{2,1,0:T(8,128)(2,1)}), bf16[4,64,1024]{2,1,0:T(8,128)(2,1)S(1)}, u32[]{:S(2)}, u32[]{:S(2)}) async-start(bf16[4,64,1024]{2,1,0:T(8,128)(2,1)} %copy-done.1), calls=%async_computation.2 | async-start | bytes 1048576 | tf_op jit(solution)/shard_map/all_to_all | solution.py:159
  55.8 0.8 slice_bitcast_fusion.12
  56.6 1.0 pad_maximum_fusion.2
  57.6 1.1 collective-permute-start.3
  58.7 1.0 collective-permute-start.5
  59.7 0.8 pad_maximum_fusion.7
  60.6 1.6 %collective-permute-start.4 = (bf16[48,1024]{1,0:T(8,128)(2,1)S(1)}, bf16[48,1024]{1,0:T(8,128)(2,1)S(1)}, u32[]{:S(2)}, u32[]{:S(2)}) collective-permute-start(bf16[48,1024]{1,0:T(8,128)(2,1)S(1)} %pad_maximum_fusion.7), channel_id=1, source_target_pairs={{0,32},{16,48},{32,0},{48,16},{1,33},{17,49},{33,1},{49,17},{2,34}... | collective-permute-start | bytes 294920 | tf_op jit(solution)/shard_map/ppermute | solution.py:165
  62.2 4.6 %collective-permute-done.4 = bf16[48,1024]{1,0:T(8,128)(2,1)S(1)} collective-permute-done((bf16[48,1024]{1,0:T(8,128)(2,1)S(1)}, bf16[48,1024]{1,0:T(8,128)(2,1)S(1)}, u32[]{:S(2)}, u32[]{:S(2)}) %collective-permute-start.4) | collective-permute-done | bytes 98336 | tf_op jit(solution)/shard_map/ppermute | solution.py:165
  67.6 1.6 %collective-permute-done.6 = bf16[4,48,1024]{2,1,0:T(8,128)(2,1)S(1)} collective-permute-done((bf16[4,48,1024]{2,1,0:T(8,128)(2,1)S(1)}, bf16[4,48,1024]{2,1,0:T(8,128)(2,1)S(1)}, u32[]{:S(2)}, u32[]{:S(2)}) %collective-permute-start.6) | collective-permute-done | bytes 393248 | tf_op jit(solution)/shard_map/ppermute | solution.py:155
  69.5 0.8 copy.21
  70.3 1.3 %fusion.8 = f32[512,1024]{1,0:T(8,128)S(1)} fusion(bf16[128,512]{1,0:T(8,128)(2,1)S(1)} %bitcast.141, bf16[32,1024]{1,0:T(8,128)(2,1)S(1)} %get-tuple-element.57, bf16[32,1024]{1,0:T(8,128)(2,1)} %collective-permute-done.1, bf16[32,1024]{1,0:T(8,128)(2,1)S(1)} %get-tuple-element.73, bf16[32,1024]{1,0:T(8,128)(2,1)S(1)} %get-tuple-element.53), kind=kOutput, calls=%fused_computation.17 | convolution fusion | flops 135266304 | bytes 2490368 | tf_op jit(solution)/shard_map/dot_general | solution.py:253
  71.9 11.6 %all-to-all-start.3 = ((bf16[32,48,128]{2,1,0:T(8,128)(2,1)}), bf16[32,48,128]{2,1,0:T(8,128)(2,1)S(1)}, u32[]{:S(2)}, u32[]{:S(2)}) async-start(bf16[32,48,128]{2,1,0:T(8,128)(2,1)} %bitcast.34), calls=%async_computation.3 | async-start | bytes 786432 | tf_op jit(solution)/shard_map/all_to_all | solution.py:159
  83.6 1.2 %fusion.1 = bf16[4,64,1024]{2,1,0:T(8,128)(2,1)S(1)} fusion(bf16[4,64,1024]{2,1,0:T(8,128)(2,1)} %collective-permute-done.7, f32[4,2,64,1024]{3,2,1,0:T(8,128)S(1)} %bitcast.134, s32[]{:T(128)S(6)} %select_n.89), kind=kLoop, calls=%fused_computation.3 | loop fusion | flops 786432 | bytes 2097156 | tf_op jit(solution)/shard_map/convert_element_type | solution.py:258
  84.8 3.0 %collective-permute-start.10 = (bf16[64,1024]{1,0:T(8,128)(2,1)S(1)}, bf16[64,1024]{1,0:T(8,128)(2,1)S(1)}, u32[]{:S(2)}, u32[]{:S(2)}) collective-permute-start(bf16[64,1024]{1,0:T(8,128)(2,1)S(1)} %get-tuple-element.43), channel_id=1, source_target_pairs={{0,192},{64,0},{128,64},{192,128},{1,193},{65,1},{129,65},{193,129... | collective-permute-start | bytes 393224 | tf_op jit(solution)/shard_map/ppermute | solution.py:165
  87.9 2.3 %collective-permute-start.9 = (bf16[64,1024]{1,0:T(8,128)(2,1)S(1)}, bf16[64,1024]{1,0:T(8,128)(2,1)S(1)}, u32[]{:S(2)}, u32[]{:S(2)}) collective-permute-start(bf16[64,1024]{1,0:T(8,128)(2,1)S(1)} %get-tuple-element.44), channel_id=1, source_target_pairs={{0,128},{64,192},{128,0},{192,64},{1,129},{65,193},{129,1},{193,65... | collective-permute-start | bytes 393224 | tf_op jit(solution)/shard_map/ppermute | solution.py:165
  90.6 6.2 %collective-permute-done.8 = bf16[64,1024]{1,0:T(8,128)(2,1)S(1)} collective-permute-done((bf16[64,1024]{1,0:T(8,128)(2,1)S(1)}, bf16[64,1024]{1,0:T(8,128)(2,1)S(1)}, u32[]{:S(2)}, u32[]{:S(2)}) %collective-permute-start.8) | collective-permute-done | bytes 131104 | tf_op jit(solution)/shard_map/ppermute | solution.py:165
  97.1 0.7 pad_maximum_fusion.1
  97.8 6.5 %all-to-all-start.4 = ((bf16[8,112,128]{2,1,0:T(8,128)(2,1)}), bf16[8,112,128]{2,1,0:T(8,128)(2,1)S(1)}, u32[]{:S(2)}, u32[]{:S(2)}) async-start(bf16[8,112,128]{2,1,0:T(8,128)(2,1)} %pad_maximum_fusion.1), calls=%async_computation.4 | async-start | bytes 458752 | tf_op jit(solution)/shard_map/all_to_all | solution.py:159
  104.4 3.6 %fusion = bf16[1,32,1024]{2,1,0:T(8,128)(2,1)} fusion(bf16[32,2048]{1,0:T(8,128)(2,1)S(1)} %get-tuple-element.29, bf16[2048,1024]{1,0:T(8,128)(2,1)} %param.11), kind=kOutput, calls=%fused_computation.1 | convolution fusion | flops 134250496 | bytes 4390912 | tf_op jit(solution)/shard_map/dot_general | solution.py:223
  108.0 6.5 %all-to-all-done.4 = bf16[8,112,128]{2,1,0:T(8,128)(2,1)S(1)} async-done(((bf16[8,112,128]{2,1,0:T(8,128)(2,1)}), bf16[8,112,128]{2,1,0:T(8,128)(2,1)S(1)}, u32[]{:S(2)}, u32[]{:S(2)}) %all-to-all-start.4) | async-done | bytes 229408 | tf_op jit(solution)/shard_map/all_to_all | solution.py:159
  114.6 0.8 reshape.78
  (62 shorter events, 4.4 us)
Async XLA Ops:
  0.6 10.1 %collective-permute-start = (bf16[24,32768]{1,0:T(8,128)(2,1)}, bf16[24,32768]{1,0:T(8,128)(2,1)}, u32[]{:S(2)}, u32[]{:S(2)}) collective-permute-start(bf16[24,32768]{1,0:T(8,128)(2,1)} %own_ref.1), channel_id=1, source_target_pairs={{0,8},{8,0},{1,9},{9,1},{2,10},{10,2},{3,11},{11,3},{4,12},{12,4},... | collective-permute-start | bytes 4718600 | tf_op jit(solution)/shard_map/ppermute | solution.py:155
  1.6 8.9 %copy-start.3 = (s32[1,2048]{1,0:T(1,128)S(1)}, s32[1,2048]{1,0:T(1,128)}, u32[]{:S(2)}) copy-start(s32[1,2048]{1,0:T(1,128)} %param.14) | copy-start | bytes 24580
  1.7 8.9 %copy-start.7 = (s32[1,2048,16]{1,2,0:T(8,128)S(1)}, s32[1,2048,16]{1,2,0:T(8,128)}, u32[]{:S(2)}) copy-start(s32[1,2048,16]{1,2,0:T(8,128)} %param.13) | copy-start | bytes 393220
  3.0 7.7 %copy-start = (bf16[24,32768]{1,0:T(8,128)(2,1)S(1)}, bf16[24,32768]{1,0:T(8,128)(2,1)}, u32[]{:S(2)}) copy-start(bf16[24,32768]{1,0:T(8,128)(2,1)} %own_ref.1) | copy-start | bytes 4718596
  3.0 7.7 %copy-start.4 = (s32[1,2048]{1,0:T(1,128)S(1)}, s32[1,2048]{1,0:T(1,128)}, u32[]{:S(2)}) copy-start(s32[1,2048]{1,0:T(1,128)} %param.12) | copy-start | bytes 24580
  3.0 31.4 %all-to-all-start = ((bf16[16,24,2,1024]{3,1,2,0:T(8,128)(2,1)}), bf16[16,24,2,1024]{3,1,2,0:T(8,128)(2,1)S(1)}, u32[]{:S(2)}, u32[]{:S(2)}) async-start(bf16[16,24,2,1024]{3,1,2,0:T(8,128)(2,1)} %broadcast_in_dim.26), calls=%async_computation | async-start | bytes 3145728 | tf_op jit(solution)/shard_map/all_to_all | solution.py:159
  10.5 23.8 %copy-start.6 = (bf16[1,32,1024]{2,1,0:T(8,128)(2,1)S(1)}, bf16[1,32,1024]{2,1,0:T(8,128)(2,1)}, u32[]{:S(2)}) copy-start(bf16[1,32,1024]{2,1,0:T(8,128)(2,1)} %param.17) | copy-start | bytes 196612
  34.4 14.4 %collective-permute-start.2 = (bf16[16,48,1024]{2,1,0:T(8,128)(2,1)S(1)}, bf16[16,48,1024]{2,1,0:T(8,128)(2,1)S(1)}, u32[]{:S(2)}, u32[]{:S(2)}) collective-permute-start(bf16[16,48,1024]{2,1,0:T(8,128)(2,1)S(1)} %bitcast.126), channel_id=1, source_target_pairs={{0,8},{8,0},{1,9},{9,1},{2,10},{10,2},{3,11},{11,3},{4,12},{12,4},... | collective-permute-start | bytes 4718600 | tf_op jit(solution)/shard_map/ppermute | solution.py:155
  34.4 11.3 %collective-permute-start.1 = (bf16[32,1024]{1,0:T(8,128)(2,1)S(1)}, bf16[32,1024]{1,0:T(8,128)(2,1)}, u32[]{:S(2)}, u32[]{:S(2)}) collective-permute-start(bf16[32,1024]{1,0:T(8,128)(2,1)S(1)} %bitcast.144), channel_id=1, source_target_pairs={{0,32},{16,48},{32,0},{48,16},{1,33},{17,49},{33,1},{49,17},{2,34}... | collective-permute-start | bytes 196616 | tf_op jit(solution)/shard_map/ppermute | solution.py:218
  35.4 13.5 %all-to-all-start.1 = ((bf16[16,64,96]{2,1,0:T(8,128)(2,1)}), bf16[16,64,96]{2,1,0:T(8,128)(2,1)}, u32[]{:S(2)}, u32[]{:S(2)}) async-start(bf16[16,64,96]{2,1,0:T(8,128)(2,1)} %get-tuple-element.22), calls=%async_computation.1 | async-start | bytes 524288 | tf_op jit(solution)/shard_map/all_to_all | solution.py:159
  42.1 3.6 %copy-start.5 = (s32[1,32]{1,0:T(1,128)S(1)}, s32[1,32]{1,0:T(1,128)}, u32[]{:S(2)}) copy-start(s32[1,32]{1,0:T(1,128)} %count_ref.1) | copy-start | bytes 388
  42.1 3.6 %copy-start.8 = (s32[1,32,8]{1,2,0:T(8,128)S(1)}, s32[1,32,8]{1,2,0:T(8,128)}, u32[]{:S(2)}) copy-start(s32[1,32,8]{1,2,0:T(8,128)} %param.15) | copy-start | bytes 3076
  50.9 0.8 copy-start.1
  51.7 0.7 copy-start.2
  52.3 14.4 %all-to-all-start.2 = ((bf16[4,64,1024]{2,1,0:T(8,128)(2,1)}), bf16[4,64,1024]{2,1,0:T(8,128)(2,1)S(1)}, u32[]{:S(2)}, u32[]{:S(2)}) async-start(bf16[4,64,1024]{2,1,0:T(8,128)(2,1)} %copy-done.1), calls=%async_computation.2 | async-start | bytes 1048576 | tf_op jit(solution)/shard_map/all_to_all | solution.py:159
  57.6 9.1 %collective-permute-start.3 = (bf16[80,1024]{1,0:T(8,128)(2,1)S(1)}, bf16[80,1024]{1,0:T(8,128)(2,1)S(1)}, u32[]{:S(2)}, u32[]{:S(2)}) collective-permute-start(bf16[80,1024]{1,0:T(8,128)(2,1)S(1)} %get-tuple-element.66), channel_id=1, source_target_pairs={{0,16},{16,32},{32,48},{48,0},{1,17},{17,33},{33,49},{49,1},{2,18}... | collective-permute-start | bytes 491528 | tf_op jit(solution)/shard_map/ppermute | solution.py:165
  58.7 8.1 %collective-permute-start.5 = (bf16[80,1024]{1,0:T(8,128)(2,1)S(1)}, bf16[80,1024]{1,0:T(8,128)(2,1)S(1)}, u32[]{:S(2)}, u32[]{:S(2)}) collective-permute-start(bf16[80,1024]{1,0:T(8,128)(2,1)S(1)} %get-tuple-element.65), channel_id=1, source_target_pairs={{0,48},{16,0},{32,16},{48,32},{1,49},{17,1},{33,17},{49,33},{2,50}... | collective-permute-start | bytes 491528 | tf_op jit(solution)/shard_map/ppermute | solution.py:165
  60.6 6.2 %collective-permute-start.4 = (bf16[48,1024]{1,0:T(8,128)(2,1)S(1)}, bf16[48,1024]{1,0:T(8,128)(2,1)S(1)}, u32[]{:S(2)}, u32[]{:S(2)}) collective-permute-start(bf16[48,1024]{1,0:T(8,128)(2,1)S(1)} %pad_maximum_fusion.7), channel_id=1, source_target_pairs={{0,32},{16,48},{32,0},{48,16},{1,33},{17,49},{33,1},{49,17},{2,34}... | collective-permute-start | bytes 294920 | tf_op jit(solution)/shard_map/ppermute | solution.py:165
  67.5 1.8 %collective-permute-start.6 = (bf16[4,48,1024]{2,1,0:T(8,128)(2,1)S(1)}, bf16[4,48,1024]{2,1,0:T(8,128)(2,1)S(1)}, u32[]{:S(2)}, u32[]{:S(2)}) collective-permute-start(bf16[4,48,1024]{2,1,0:T(8,128)(2,1)S(1)} %fusion.6), channel_id=1, source_target_pairs={{0,8},{8,0},{1,9},{9,1},{2,10},{10,2},{3,11},{11,3},{4,12},{12,4},... | collective-permute-start | bytes 1179656 | tf_op jit(solution)/shard_map/ppermute | solution.py:155
  71.7 11.9 %collective-permute-start.7 = (bf16[4,64,1024]{2,1,0:T(8,128)(2,1)S(1)}, bf16[4,64,1024]{2,1,0:T(8,128)(2,1)}, u32[]{:S(2)}, u32[]{:S(2)}) collective-permute-start(bf16[4,64,1024]{2,1,0:T(8,128)(2,1)S(1)} %fusion.3), channel_id=1, source_target_pairs={{0,8},{8,0},{1,9},{9,1},{2,10},{10,2},{3,11},{11,3},{4,12},{12,4},... | collective-permute-start | bytes 1572872 | tf_op jit(solution)/shard_map/ppermute | solution.py:155
  71.9 25.1 %all-to-all-start.3 = ((bf16[32,48,128]{2,1,0:T(8,128)(2,1)}), bf16[32,48,128]{2,1,0:T(8,128)(2,1)S(1)}, u32[]{:S(2)}, u32[]{:S(2)}) async-start(bf16[32,48,128]{2,1,0:T(8,128)(2,1)} %bitcast.34), calls=%async_computation.3 | async-start | bytes 786432 | tf_op jit(solution)/shard_map/all_to_all | solution.py:159
  84.8 5.8 %collective-permute-start.10 = (bf16[64,1024]{1,0:T(8,128)(2,1)S(1)}, bf16[64,1024]{1,0:T(8,128)(2,1)S(1)}, u32[]{:S(2)}, u32[]{:S(2)}) collective-permute-start(bf16[64,1024]{1,0:T(8,128)(2,1)S(1)} %get-tuple-element.43), channel_id=1, source_target_pairs={{0,192},{64,0},{128,64},{192,128},{1,193},{65,1},{129,65},{193,129... | collective-permute-start | bytes 393224 | tf_op jit(solution)/shard_map/ppermute | solution.py:165
  87.9 8.9 %collective-permute-start.8 = (bf16[64,1024]{1,0:T(8,128)(2,1)S(1)}, bf16[64,1024]{1,0:T(8,128)(2,1)S(1)}, u32[]{:S(2)}, u32[]{:S(2)}) collective-permute-start(bf16[64,1024]{1,0:T(8,128)(2,1)S(1)} %get-tuple-element.42), channel_id=1, source_target_pairs={{0,64},{64,128},{128,192},{192,0},{1,65},{65,129},{129,193},{193,1... | collective-permute-start | bytes 393224 | tf_op jit(solution)/shard_map/ppermute | solution.py:165
  87.9 8.9 %collective-permute-start.9 = (bf16[64,1024]{1,0:T(8,128)(2,1)S(1)}, bf16[64,1024]{1,0:T(8,128)(2,1)S(1)}, u32[]{:S(2)}, u32[]{:S(2)}) collective-permute-start(bf16[64,1024]{1,0:T(8,128)(2,1)S(1)} %get-tuple-element.44), channel_id=1, source_target_pairs={{0,128},{64,192},{128,0},{192,64},{1,129},{65,193},{129,1},{193,65... | collective-permute-start | bytes 393224 | tf_op jit(solution)/shard_map/ppermute | solution.py:165
  97.8 16.7 %all-to-all-start.4 = ((bf16[8,112,128]{2,1,0:T(8,128)(2,1)}), bf16[8,112,128]{2,1,0:T(8,128)(2,1)S(1)}, u32[]{:S(2)}, u32[]{:S(2)}) async-start(bf16[8,112,128]{2,1,0:T(8,128)(2,1)} %pad_maximum_fusion.1), calls=%async_computation.4 | async-start | bytes 458752 | tf_op jit(solution)/shard_map/all_to_all | solution.py:159
